TPU v7x, 512 devices: a whole 4x8x8 slice. The times are simulated.
512 devices in a mesh: ta: 8 (over x, y_lo), gz: 8 (over y_hi, core), gy: 8 (over z).
Axes of the slice: x: 4, y: 8 (y_hi: 4, y_lo: 2; y = y_hi * 2 + y_lo), z: 8, core: 2. Of those that a mesh axis runs over, the one named last changes fastest.
Arguments:
- quark_field: float32 [4, 3, 16, 32, 16, 128], P(None, None, 'ta', 'gz', 'gy'), may hold values from -6 to 6
- gauge_links: float32 [4, 3, 3, 16, 32, 16, 128], P(None, None, None, 'ta', 'gz', 'gy'), may hold values from -3 to 3
Outputs:
- result_field: float32 [4, 3, 16, 32, 16, 128], P(None, None, 'ta', 'gz', 'gy')
- link_force: float32 [4, 3, 3, 16, 32, 16, 128], P(None, None, None, 'ta', 'gz', 'gy')
All inputs are finite; a program needn't handle non-finite values.
Results may differ from a plain program's by a relative error of at most 0.0001.
Values sent between devices are 32-bit elements; how exact they have to be, the bound alone decides.
A program may use at most 64 MiB of HBM per device.

v0:
```python
import jax
import jax.numpy as jnp
import numpy as np
from jax import lax
from jax.sharding import PartitionSpec as P

hopping_kappa = 0.125


def with_halo(cells, sides, width):
    for axis, dim in sides:
        count = lax.axis_size(axis)
        head = lax.slice_in_dim(cells, 0, width, axis=dim)
        tail = lax.slice_in_dim(cells, cells.shape[dim] - width, cells.shape[dim], axis=dim)
        cells = jnp.concatenate(
            [
                lax.ppermute(tail, axis, [(i, (i + 1) % count) for i in range(count)]),
                cells,
                lax.ppermute(head, axis, [((i + 1) % count, i) for i in range(count)]),
            ],
            axis=dim,
        )
    return cells


def shifted(value, axis, steps):
    count = lax.axis_size(axis)
    pairs = [(source, (source + steps) % count) for source in range(count)]
    return lax.ppermute(value, axis, pairs)


def block_matrix(upper_left, upper_right, lower_left, lower_right):
    upper = np.concatenate([upper_left, upper_right], axis=1)
    lower = np.concatenate([lower_left, lower_right], axis=1)
    return np.concatenate([upper, lower], axis=0)


def gamma_tables():
    paulis = [
        np.array([[0, 1], [1, 0]], dtype=complex),
        np.array([[0, -1j], [1j, 0]], dtype=complex),
        np.array([[1, 0], [0, -1]], dtype=complex),
    ]
    zero_block = np.zeros((2, 2), dtype=complex)
    unit_block = np.eye(2, dtype=complex)
    gammas = [
        block_matrix(zero_block, -1j * pauli_matrix, 1j * pauli_matrix, zero_block)
        for pauli_matrix in paulis
    ]
    gammas.append(block_matrix(zero_block, unit_block, unit_block, zero_block))
    stacked = np.stack(gammas)
    return (stacked.real.astype(np.float32), stacked.imag.astype(np.float32))


def mix_apply(table, part):
    factor = jnp.asarray(table, dtype=part.dtype).reshape((4, 4) + (1,) * (part.ndim - 1))
    return jnp.sum(factor * part[None], axis=1)


def spin_project(direction, parity, part_real, part_imag):
    table_real, table_imag = gamma_tables()
    mix_real = parity * table_real[direction]
    mix_imag = parity * table_imag[direction]
    new_real = part_real + mix_apply(mix_real, part_real) - mix_apply(mix_imag, part_imag)
    new_imag = part_imag + mix_apply(mix_real, part_imag) + mix_apply(mix_imag, part_real)
    return (new_real, new_imag)


def colour_times(link, part):
    return jnp.sum(link[None] * part[:, None], axis=2)


def link_apply(link_real, link_imag, part_real, part_imag):
    new_real = colour_times(link_real, part_real) - colour_times(link_imag, part_imag)
    new_imag = colour_times(link_real, part_imag) + colour_times(link_imag, part_real)
    return (new_real, new_imag)


def adjoint_apply(link_real, link_imag, part_real, part_imag):
    flip_real = jnp.swapaxes(link_real, 0, 1)
    flip_imag = jnp.swapaxes(link_imag, 0, 1)
    new_real = colour_times(flip_real, part_real) + colour_times(flip_imag, part_imag)
    new_imag = colour_times(flip_real, part_imag) - colour_times(flip_imag, part_real)
    return (new_real, new_imag)


def spin_outer(left, right):
    return jnp.sum(left[:, :, None] * right[:, None, :], axis=0)


def outer_product(left_real, left_imag, right_real, right_imag):
    new_real = spin_outer(left_real, right_real) + spin_outer(left_imag, right_imag)
    new_imag = spin_outer(left_imag, right_real) - spin_outer(left_real, right_imag)
    return (new_real, new_imag)


def matrix_times(left, right):
    return jnp.sum(left[:, :, None] * right[None, :, :], axis=1)


def times_link(link_real, link_imag, matrix_real, matrix_imag):
    new_real = matrix_times(link_real, matrix_real) - matrix_times(link_imag, matrix_imag)
    new_imag = matrix_times(link_real, matrix_imag) + matrix_times(link_imag, matrix_real)
    return (new_real, new_imag)


def traceless_part(whole_real, whole_imag):
    anti_real = 0.5 * (whole_real - jnp.swapaxes(whole_real, 0, 1))
    anti_imag = 0.5 * (whole_imag + jnp.swapaxes(whole_imag, 0, 1))
    trace_third = (whole_imag[0, 0] + whole_imag[1, 1] + whole_imag[2, 2]) / 3.0
    identity = jnp.eye(3, dtype=whole_imag.dtype)[:, :, None, None, None, None]
    return (anti_real, anti_imag - identity * trace_third)


def roll_cells(merged, stride, local_x):
    shaped = merged.reshape(merged.shape[:-1] + (2, local_x))
    return jnp.roll(shaped, -stride, axis=-1).reshape(merged.shape)


def time_signs(padded):
    first_rank = lax.axis_index("ta") == 0
    last_rank = lax.axis_index("ta") == lax.axis_size("ta") - 1
    lower_sign = jnp.where(first_rank, -1.0, 1.0).astype(padded.dtype)
    upper_sign = jnp.where(last_rank, -1.0, 1.0).astype(padded.dtype)
    middle_ones = jnp.ones((padded.shape[2] - 2,), padded.dtype)
    factor = jnp.concatenate([lower_sign[None], middle_ones, upper_sign[None]])
    return padded * factor[:, None, None, None]


def split_parts(merged, local_x):
    return (merged[..., :local_x], merged[..., local_x:])


def body(quark_field, gauge_links):
    local_x = quark_field.shape[-1] // 2
    joined = with_halo(quark_field, (("ta", 2), ("gz", 3), ("gy", 4)), 1)
    pad_t = joined[:, :, :, 1:-1, 1:-1, :]
    pad_z = joined[:, :, 1:-1, :, 1:-1, :]
    pad_y = joined[:, :, 1:-1, 1:-1, :, :]
    pad_t = time_signs(pad_t)
    pads = [None, pad_y, pad_z, pad_t]

    def quark_neighbour(direction, stride):
        if direction == 0:
            return roll_cells(quark_field, stride, local_x)
        dim = 5 - direction
        count = quark_field.shape[dim]
        return lax.slice_in_dim(pads[direction], 1 + stride, 1 + stride + count, axis=dim)

    quark_real, quark_imag = split_parts(quark_field, local_x)
    back_links = [roll_cells(gauge_links[0], -1, local_x)]
    below_y = shifted(gauge_links[1][:, :, :, :, -1:, :], "gy", 1)
    back_links.append(jnp.concatenate([below_y, gauge_links[1][:, :, :, :, :-1, :]], axis=4))
    below_z = shifted(gauge_links[2][:, :, :, -1:, :, :], "gz", 1)
    back_links.append(jnp.concatenate([below_z, gauge_links[2][:, :, :, :-1, :, :]], axis=3))
    below_t = shifted(gauge_links[3][:, :, -1:, :, :, :], "ta", 1)
    back_links.append(jnp.concatenate([below_t, gauge_links[3][:, :, :-1, :, :, :]], axis=2))
    gauge_real, gauge_imag = split_parts(gauge_links, local_x)
    hop_real = jnp.zeros_like(quark_real)
    hop_imag = jnp.zeros_like(quark_imag)
    for direction in range(4):
        ahead_real, ahead_imag = split_parts(quark_neighbour(direction, 1), local_x)
        moved_real, moved_imag = link_apply(
            gauge_real[direction], gauge_imag[direction], ahead_real, ahead_imag
        )
        term_real, term_imag = spin_project(direction, -1.0, moved_real, moved_imag)
        hop_real = hop_real + term_real
        hop_imag = hop_imag + term_imag
        behind_real, behind_imag = split_parts(quark_neighbour(direction, -1), local_x)
        back_real, back_imag = split_parts(back_links[direction], local_x)
        moved_real, moved_imag = adjoint_apply(back_real, back_imag, behind_real, behind_imag)
        term_real, term_imag = spin_project(direction, 1.0, moved_real, moved_imag)
        hop_real = hop_real + term_real
        hop_imag = hop_imag + term_imag
    result_real = quark_real - hopping_kappa * hop_real
    result_imag = quark_imag - hopping_kappa * hop_imag
    result_field = jnp.concatenate([result_real, result_imag], axis=-1)
    upper_y = shifted(result_field[:, :, :, :, :1], "gy", -1)
    upper_z = shifted(result_field[:, :, :, :1], "gz", -1)
    upper_t = shifted(result_field[:, :, :1], "ta", -1)
    last_rank = lax.axis_index("ta") == lax.axis_size("ta") - 1
    upper_sign = jnp.where(last_rank, -1.0, 1.0).astype(result_field.dtype)
    later_fields = [
        roll_cells(result_field, 1, local_x),
        jnp.concatenate([result_field[:, :, :, :, 1:], upper_y], axis=4),
        jnp.concatenate([result_field[:, :, :, 1:], upper_z], axis=3),
        jnp.concatenate([result_field[:, :, 1:], upper_sign * upper_t], axis=2),
    ]
    forces = []
    for direction in range(4):
        ahead_real, ahead_imag = split_parts(quark_neighbour(direction, 1), local_x)
        ahead_real, ahead_imag = spin_project(direction, -1.0, ahead_real, ahead_imag)
        first_real, first_imag = outer_product(ahead_real, ahead_imag, result_real, result_imag)
        later_real, later_imag = split_parts(later_fields[direction], local_x)
        later_real, later_imag = spin_project(direction, 1.0, later_real, later_imag)
        second_real, second_imag = outer_product(later_real, later_imag, quark_real, quark_imag)
        whole_real, whole_imag = times_link(
            gauge_real[direction],
            gauge_imag[direction],
            first_real + second_real,
            first_imag + second_imag,
        )
        force_real, force_imag = traceless_part(whole_real, whole_imag)
        forces.append(
            jnp.concatenate([hopping_kappa * force_real, hopping_kappa * force_imag], axis=-1)
        )
    return (result_field, jnp.stack(forces))


def solution(mesh):
    in_specs = (P(None, None, "ta", "gz", "gy", None), P(None, None, None, "ta", "gz", "gy", None))
    out_specs = (P(None, None, "ta", "gz", "gy", None), P(None, None, None, "ta", "gz", "gy", None))
    return jax.shard_map(body, mesh=mesh, in_specs=in_specs, out_specs=out_specs, check_vma=False)
```

profile of v0, /device:TPU:1, one launch (start us, length us, event | category | flops | bytes accessed | tf_op | source)
XLA Modules:
  0.0 86.2 jit_solution(1449726506603563111)
XLA Ops:
  0.6 1.0 %copy.92 = f32[4,3,2,4,2,128]{5,3,4,2,1,0:T(4,128)S(1)} copy(f32[4,3,2,4,2,128]{5,4,3,2,1,0:T(2,128)} %param.66) | data formatting | bytes 196608 | tf_op args[0]
  1.6 4.0 %collective-permute-start = (f32[4,3,1,4,2,128]{5,3,4,2,1,0:T(4,128)S(1)}, f32[4,3,1,4,2,128]{5,3,4,2,1,0:T(4,128)S(1)}, u32[]{:S(2)}, u32[]{:S(2)}) collective-permute-start(f32[4,3,1,4,2,128]{5,3,4,2,1,0:T(4,128)S(1)} %get-tuple-element.252), channel_id=1, source_target_pairs={{0,64},{64,128},{128,192},{192,256},{256,320},{320,384},{384,448},... | collective-permute-start | bytes 147464 | tf_op jit(solution)/shard_map/ppermute | solution.py:17
  5.7 4.1 %collective-permute-start.1 = (f32[4,3,1,4,2,128]{5,3,4,2,1,0:T(4,128)S(1)}, f32[4,3,1,4,2,128]{5,3,4,2,1,0:T(4,128)S(1)}, u32[]{:S(2)}, u32[]{:S(2)}) collective-permute-start(f32[4,3,1,4,2,128]{5,3,4,2,1,0:T(4,128)S(1)} %get-tuple-element.251), channel_id=1, source_target_pairs={{64,0},{128,64},{192,128},{256,192},{320,256},{384,320},{448,384},... | collective-permute-start | bytes 147464 | tf_op jit(solution)/shard_map/ppermute | solution.py:19
  9.9 4.1 %collective-permute-start.5 = (f32[3,3,2,4,1,128]{5,4,3,2,1,0:T(1,128)S(1)}, f32[3,3,2,4,1,128]{5,4,3,2,1,0:T(1,128)S(1)}, u32[]{:S(2)}, u32[]{:S(2)}) collective-permute-start(f32[3,3,2,4,1,128]{5,4,3,2,1,0:T(1,128)S(1)} %get-tuple-element.257), channel_id=1, source_target_pairs={{0,1},{1,2},{2,3},{3,4},{4,5},{5,6},{6,7},{7,0},{8,9},{9,10},{10,1... | collective-permute-start | bytes 110600 | tf_op jit(solution)/shard_map/ppermute | solution.py:29
  14.0 0.6 slice.431
  14.6 5.6 %collective-permute-start.7 = (f32[3,3,2,1,2,128]{5,4,3,2,1,0:T(2,128)}, f32[3,3,2,1,2,128]{5,4,3,2,1,0:T(2,128)S(1)}, u32[]{:S(2)}, u32[]{:S(2)}) collective-permute-start(f32[3,3,2,1,2,128]{5,4,3,2,1,0:T(2,128)} %slice.431), channel_id=1, source_target_pairs={{0,8},{8,16},{16,24},{24,32},{32,40},{40,48},{48,56},{56,0},{1,9},... | collective-permute-start | bytes 55304 | tf_op jit(solution)/shard_map/ppermute | solution.py:29
  20.2 2.1 %collective-permute-start.8 = (f32[3,3,1,4,2,128]{5,4,3,2,1,0:T(2,128)S(1)}, f32[3,3,1,4,2,128]{5,4,3,2,1,0:T(2,128)S(1)}, u32[]{:S(2)}, u32[]{:S(2)}) collective-permute-start(f32[3,3,1,4,2,128]{5,4,3,2,1,0:T(2,128)S(1)} %get-tuple-element.263), channel_id=1, source_target_pairs={{0,64},{64,128},{128,192},{192,256},{256,320},{320,384},{384,448},... | collective-permute-start | bytes 110600 | tf_op jit(solution)/shard_map/ppermute | solution.py:29
  22.3 0.4 slice_bitcast_fusion.9
  22.9 0.3 fusion.29
  23.1 0.3 fusion.30
  23.7 0.2 slice.413
  23.9 0.2 pad_maximum_fusion.5
  24.5 0.5 pad_maximum_fusion.2
  24.9 0.2 reshape.401
  25.4 0.2 reshape.404
  26.0 0.4 multiply_reduce_fusion.105
  26.5 0.4 multiply_reduce_fusion.109
  27.0 0.7 copy-done.13
  27.7 0.5 multiply_reduce_fusion.22
  28.3 0.7 copy-done.7
  29.0 0.3 multiply_reduce_fusion.46
  29.9 0.2 fusion.2
  30.6 1.9 %collective-permute-start.2 = (f32[4,3,4,1,2,128]{5,3,4,2,1,0:T(1,128)S(1)}, f32[4,3,4,1,2,128]{5,3,4,2,1,0:T(1,128)S(1)}, u32[]{:S(2)}, u32[]{:S(2)}) collective-permute-start(f32[4,3,4,1,2,128]{5,3,4,2,1,0:T(1,128)S(1)} %get-tuple-element.229), channel_id=1, source_target_pairs={{0,8},{8,16},{16,24},{24,32},{32,40},{40,48},{48,56},{56,0},{1,9},... | collective-permute-start | bytes 147464 | tf_op jit(solution)/shard_map/ppermute | solution.py:17
  32.5 2.7 %collective-permute-start.3 = (f32[4,3,4,1,2,128]{5,3,4,2,1,0:T(1,128)S(1)}, f32[4,3,4,1,2,128]{5,3,4,2,1,0:T(1,128)S(1)}, u32[]{:S(2)}, u32[]{:S(2)}) collective-permute-start(f32[4,3,4,1,2,128]{5,3,4,2,1,0:T(1,128)S(1)} %get-tuple-element.228), channel_id=1, source_target_pairs={{8,0},{16,8},{24,16},{32,24},{40,32},{48,40},{56,48},{0,56},{9,1},... | collective-permute-start | bytes 147464 | tf_op jit(solution)/shard_map/ppermute | solution.py:19
  35.5 0.4 multiply_reduce_fusion.87
  36.0 0.7 copy-done.12
  36.7 0.5 multiply_reduce_fusion.2
  37.4 0.4 multiply_reduce_fusion.83
  37.9 0.7 copy-done.4
  38.6 0.3 multiply_reduce_fusion.36
  38.9 1.2 %collective-permute-done.3 = f32[4,3,4,1,2,128]{5,3,4,2,1,0:T(1,128)S(1)} collective-permute-done((f32[4,3,4,1,2,128]{5,3,4,2,1,0:T(1,128)S(1)}, f32[4,3,4,1,2,128]{5,3,4,2,1,0:T(1,128)S(1)}, u32[]{:S(2)}, u32[]{:S(2)}) %collective-permute-start.3) | collective-permute-done | bytes 49184 | tf_op jit(solution)/shard_map/ppermute | solution.py:19
  40.2 8.3 %collective-permute-start.4 = (f32[4,3,4,6,1,128]{5,3,4,2,1,0:T(8,128)S(1)}, f32[4,3,4,6,1,128]{5,3,4,2,1,0:T(8,128)S(1)}, u32[]{:S(2)}, u32[]{:S(2)}) collective-permute-start(f32[4,3,4,6,1,128]{5,3,4,2,1,0:T(8,128)S(1)} %get-tuple-element.194), channel_id=1, source_target_pairs={{1,0},{2,1},{3,2},{4,3},{5,4},{6,5},{7,6},{0,7},{9,8},{10,9},{11,1... | collective-permute-start | bytes 442376 | tf_op jit(solution)/shard_map/ppermute | solution.py:19
  48.6 2.1 %collective-permute-start.6 = (f32[4,3,4,6,1,128]{5,3,4,2,1,0:T(8,128)S(1)}, f32[4,3,4,6,1,128]{5,3,4,2,1,0:T(8,128)S(1)}, u32[]{:S(2)}, u32[]{:S(2)}) collective-permute-start(f32[4,3,4,6,1,128]{5,3,4,2,1,0:T(8,128)S(1)} %get-tuple-element.195), channel_id=1, source_target_pairs={{0,1},{1,2},{2,3},{3,4},{4,5},{5,6},{6,7},{7,0},{8,9},{9,10},{10,1... | collective-permute-start | bytes 442376 | tf_op jit(solution)/shard_map/ppermute | solution.py:17
  50.7 0.2 pad_maximum_fusion.12
  50.9 0.4 multiply_reduce_fusion.93
  51.4 0.6 copy-done.10
  52.0 1.0 %multiply_reduce_fusion.40 = (f32[4,3,2,4,2,64]{5,3,4,2,1,0:T(4,128)S(1)}, f32[4,3,2,4,2,64]{5,3,4,2,1,0:T(4,128)S(1)}, f32[4,3,2,4,2,64]{5,3,4,2,1,0:T(4,128)S(...) fusion(f32[4,3,2,4,2,64]{5,3,4,2,1,0:T(4,128)S(1)} %add.438, ...), kind=kLoop, calls=%fused_computation.41 | loop fusion | flops 688128 | bytes 589952 | tf_op jit(solution)/shard_map/reduce_sum | solution.py:57
  53.1 5.1 %collective-permute-done.6 = f32[4,3,4,6,1,128]{5,3,4,2,1,0:T(8,128)S(1)} collective-permute-done((f32[4,3,4,6,1,128]{5,3,4,2,1,0:T(8,128)S(1)}, f32[4,3,4,6,1,128]{5,3,4,2,1,0:T(8,128)S(1)}, u32[]{:S(2)}, u32[]{:S(2)}) %collective-permute-start.6) | collective-permute-done | bytes 147488 | tf_op jit(solution)/shard_map/ppermute | solution.py:17
  58.3 0.4 pad_maximum_fusion.20
  58.7 0.4 multiply_reduce_fusion.101
  59.1 0.9 %multiply_reduce_fusion.89 = (f32[4,3,2,4,2,64]{5,3,4,2,1,0:T(4,128)S(1)}, f32[4,3,2,4,2,64]{5,3,4,2,1,0:T(4,128)S(1)}, f32[4,3,2,4,2,64]{5,3,4,2,1,0:T(4,128)S(...) fusion(f32[4,3,2,4,2,64]{5,3,4,2,1,0:T(4,128)S(1)} %get-tuple-e, ...), kind=kLoop, calls=%fused_computation.91 | loop fusion | flops 491520 | bytes 737280 | tf_op jit(solution)/shard_map/reduce_sum | solution.py:70
  60.2 0.6 copy-done.8
  60.8 1.0 %multiply_reduce_fusion.44 = (f32[4,3,2,4,2,64]{5,3,4,2,1,0:T(4,128)S(1)}, f32[4,3,2,4,2,64]{5,3,4,2,1,0:T(4,128)S(1)}, f32[4,3,2,4,2,64]{5,3,4,2,1,0:T(4,128)S(...) fusion(f32[4,3,2,4,2,64]{5,3,4,2,1,0:T(4,128)S(1)} %add.432, ...), kind=kLoop, calls=%fused_computation.45 | loop fusion | flops 688128 | bytes 589952 | tf_op jit(solution)/shard_map/reduce_sum | solution.py:57
  61.9 0.5 multiply_reduce_fusion.42
  62.6 0.5 multiply_reduce_fusion.38
  63.1 0.3 multiply_subtract_fusion.1
  63.5 0.3 multiply_subtract_fusion
  64.4 0.7 copy.154
  65.1 5.1 %collective-permute-start.11 = (f32[4,3,1,4,2,128]{5,3,4,2,1,0:T(4,128)S(1)}, f32[4,3,1,4,2,128]{5,3,4,2,1,0:T(4,128)S(1)}, u32[]{:S(2)}, u32[]{:S(2)}) collective-permute-start(f32[4,3,1,4,2,128]{5,3,4,2,1,0:T(4,128)S(1)} %get-tuple-element.220), channel_id=1, source_target_pairs={{0,448},{64,0},{128,64},{192,128},{256,192},{320,256},{384,320},{4... | collective-permute-start | bytes 147464 | tf_op jit(solution)/shard_map/ppermute | solution.py:29
  70.3 3.2 %collective-permute-start.10 = (f32[4,3,2,1,2,128]{5,3,4,2,1,0:T(1,128)S(1)}, f32[4,3,2,1,2,128]{5,3,4,2,1,0:T(1,128)S(1)}, u32[]{:S(2)}, u32[]{:S(2)}) collective-permute-start(f32[4,3,2,1,2,128]{5,3,4,2,1,0:T(1,128)S(1)} %fusion.17), channel_id=1, source_target_pairs={{0,56},{8,0},{16,8},{24,16},{32,24},{40,32},{48,40},{56,48},{1,57}... | collective-permute-start | bytes 73736 | tf_op jit(solution)/shard_map/ppermute | solution.py:29
  73.5 2.7 %collective-permute-start.9 = (f32[4,3,2,4,1,128]{5,3,4,2,1,0:T(4,128)S(1)}, f32[4,3,2,4,1,128]{5,3,4,2,1,0:T(4,128)S(1)}, u32[]{:S(2)}, u32[]{:S(2)}) collective-permute-start(f32[4,3,2,4,1,128]{5,3,4,2,1,0:T(4,128)S(1)} %get-tuple-element.222), channel_id=1, source_target_pairs={{0,7},{1,0},{2,1},{3,2},{4,3},{5,4},{6,5},{7,6},{8,15},{9,8},{10,9... | collective-permute-start | bytes 147464 | tf_op jit(solution)/shard_map/ppermute | solution.py:29
  76.1 0.3 slice.444
  76.4 0.3 pad_maximum_fusion.4
  77.0 0.3 multiply_reduce_fusion.20
  77.5 1.5 %multiply_reduce_fusion.74 = (f32[3,3,2,4,2,64]{5,3,4,2,1,0:T(4,128)S(1)}, f32[3,3,2,4,2,64]{5,3,4,2,1,0:T(4,128)S(1)}, f32[3,3,2,4,2,64]{5,3,4,2,1,0:T(4,128)S(...) fusion(f32[4,3,2,4,2,64]{5,3,4,2,1,0:T(4,128)S(1)} %multiply_su, ...), kind=kLoop, calls=%fused_computation.76 | loop fusion | flops 1032192 | bytes 1081344 | tf_op jit(solution)/shard_map/reduce_sum | solution.py:88
  79.3 0.5 multiply_reduce_fusion.4
  80.0 0.3 multiply_reduce_fusion
  80.6 0.6 multiply_reduce_fusion.12
  81.3 1.5 %multiply_reduce_fusion.72 = (f32[3,3,2,4,2,64]{5,3,4,2,1,0:T(4,128)S(1)}, f32[3,3,2,4,2,64]{5,3,4,2,1,0:T(4,128)S(1)}, f32[3,3,2,4,2,64]{5,3,4,2,1,0:T(4,128)S(...) fusion(f32[4,3,2,4,2,64]{5,3,4,2,1,0:T(4,128)S(1)} %get-tuple-e, ...), kind=kLoop, calls=%fused_computation.74 | loop fusion | flops 1032192 | bytes 1081344 | tf_op jit(solution)/shard_map/reduce_sum | solution.py:88
  82.9 0.3 multiply_reduce_fusion.126
  83.3 0.3 multiply_reduce_fusion.123
  83.7 0.3 multiply_reduce_fusion.115
  84.1 0.3 multiply_reduce_fusion.119
  85.3 0.9 %copy.155 = f32[4,3,3,2,4,2,128]{6,5,4,3,2,1,0:T(2,128)} copy(f32[4,3,3,2,4,2,128]{6,4,5,3,2,1,0:T(4,128)S(1)} %pad_maximum_fusion.1) | data formatting | bytes 589824
  (146 shorter events, 7.1 us)
Async XLA Ops:
  0.6 9.2 %copy-start = (f32[4,3,3,2,4,2,128]{6,5,4,3,2,1,0:T(2,128)S(1)}, f32[4,3,3,2,4,2,128]{6,5,4,3,2,1,0:T(2,128)}, u32[]{:S(2)}) copy-start(f32[4,3,3,2,4,2,128]{6,5,4,3,2,1,0:T(2,128)} %param.67) | copy-start | bytes 884740
  1.6 28.8 %collective-permute-start = (f32[4,3,1,4,2,128]{5,3,4,2,1,0:T(4,128)S(1)}, f32[4,3,1,4,2,128]{5,3,4,2,1,0:T(4,128)S(1)}, u32[]{:S(2)}, u32[]{:S(2)}) collective-permute-start(f32[4,3,1,4,2,128]{5,3,4,2,1,0:T(4,128)S(1)} %get-tuple-element.252), channel_id=1, source_target_pairs={{0,64},{64,128},{128,192},{192,256},{256,320},{320,384},{384,448},... | collective-permute-start | bytes 147464 | tf_op jit(solution)/shard_map/ppermute | solution.py:17
  5.7 24.8 %collective-permute-start.1 = (f32[4,3,1,4,2,128]{5,3,4,2,1,0:T(4,128)S(1)}, f32[4,3,1,4,2,128]{5,3,4,2,1,0:T(4,128)S(1)}, u32[]{:S(2)}, u32[]{:S(2)}) collective-permute-start(f32[4,3,1,4,2,128]{5,3,4,2,1,0:T(4,128)S(1)} %get-tuple-element.251), channel_id=1, source_target_pairs={{64,0},{128,64},{192,128},{256,192},{320,256},{384,320},{448,384},... | collective-permute-start | bytes 147464 | tf_op jit(solution)/shard_map/ppermute | solution.py:19
  9.9 20.0 %collective-permute-start.5 = (f32[3,3,2,4,1,128]{5,4,3,2,1,0:T(1,128)S(1)}, f32[3,3,2,4,1,128]{5,4,3,2,1,0:T(1,128)S(1)}, u32[]{:S(2)}, u32[]{:S(2)}) collective-permute-start(f32[3,3,2,4,1,128]{5,4,3,2,1,0:T(1,128)S(1)} %get-tuple-element.257), channel_id=1, source_target_pairs={{0,1},{1,2},{2,3},{3,4},{4,5},{5,6},{6,7},{7,0},{8,9},{9,10},{10,1... | collective-permute-start | bytes 110600 | tf_op jit(solution)/shard_map/ppermute | solution.py:29
  14.6 15.1 %collective-permute-start.7 = (f32[3,3,2,1,2,128]{5,4,3,2,1,0:T(2,128)}, f32[3,3,2,1,2,128]{5,4,3,2,1,0:T(2,128)S(1)}, u32[]{:S(2)}, u32[]{:S(2)}) collective-permute-start(f32[3,3,2,1,2,128]{5,4,3,2,1,0:T(2,128)} %slice.431), channel_id=1, source_target_pairs={{0,8},{8,16},{16,24},{24,32},{32,40},{40,48},{48,56},{56,0},{1,9},... | collective-permute-start | bytes 55304 | tf_op jit(solution)/shard_map/ppermute | solution.py:29
  20.2 2.4 %copy-start.1 = (f32[4,3,2,4,2,128]{5,4,3,2,1,0:T(2,128)S(1)}, f32[4,3,2,4,2,128]{5,4,3,2,1,0:T(2,128)}, u32[]{:S(2)}) copy-start(f32[4,3,2,4,2,128]{5,4,3,2,1,0:T(2,128)} %param.66) | copy-start | bytes 294916
  20.2 9.9 %collective-permute-start.8 = (f32[3,3,1,4,2,128]{5,4,3,2,1,0:T(2,128)S(1)}, f32[3,3,1,4,2,128]{5,4,3,2,1,0:T(2,128)S(1)}, u32[]{:S(2)}, u32[]{:S(2)}) collective-permute-start(f32[3,3,1,4,2,128]{5,4,3,2,1,0:T(2,128)S(1)} %get-tuple-element.263), channel_id=1, source_target_pairs={{0,64},{64,128},{128,192},{192,256},{256,320},{320,384},{384,448},... | collective-permute-start | bytes 110600 | tf_op jit(solution)/shard_map/ppermute | solution.py:29
  27.0 0.7 copy-start.13
  28.3 0.7 copy-start.7
  30.6 8.3 %collective-permute-start.2 = (f32[4,3,4,1,2,128]{5,3,4,2,1,0:T(1,128)S(1)}, f32[4,3,4,1,2,128]{5,3,4,2,1,0:T(1,128)S(1)}, u32[]{:S(2)}, u32[]{:S(2)}) collective-permute-start(f32[4,3,4,1,2,128]{5,3,4,2,1,0:T(1,128)S(1)} %get-tuple-element.229), channel_id=1, source_target_pairs={{0,8},{8,16},{16,24},{24,32},{32,40},{40,48},{48,56},{56,0},{1,9},... | collective-permute-start | bytes 147464 | tf_op jit(solution)/shard_map/ppermute | solution.py:17
  32.5 7.6 %collective-permute-start.3 = (f32[4,3,4,1,2,128]{5,3,4,2,1,0:T(1,128)S(1)}, f32[4,3,4,1,2,128]{5,3,4,2,1,0:T(1,128)S(1)}, u32[]{:S(2)}, u32[]{:S(2)}) collective-permute-start(f32[4,3,4,1,2,128]{5,3,4,2,1,0:T(1,128)S(1)} %get-tuple-element.228), channel_id=1, source_target_pairs={{8,0},{16,8},{24,16},{32,24},{40,32},{48,40},{56,48},{0,56},{9,1},... | collective-permute-start | bytes 147464 | tf_op jit(solution)/shard_map/ppermute | solution.py:19
  36.0 0.7 copy-start.12
  37.9 0.7 copy-start.4
  40.2 12.9 %collective-permute-start.4 = (f32[4,3,4,6,1,128]{5,3,4,2,1,0:T(8,128)S(1)}, f32[4,3,4,6,1,128]{5,3,4,2,1,0:T(8,128)S(1)}, u32[]{:S(2)}, u32[]{:S(2)}) collective-permute-start(f32[4,3,4,6,1,128]{5,3,4,2,1,0:T(8,128)S(1)} %get-tuple-element.194), channel_id=1, source_target_pairs={{1,0},{2,1},{3,2},{4,3},{5,4},{6,5},{7,6},{0,7},{9,8},{10,9},{11,1... | collective-permute-start | bytes 442376 | tf_op jit(solution)/shard_map/ppermute | solution.py:19
  48.6 9.7 %collective-permute-start.6 = (f32[4,3,4,6,1,128]{5,3,4,2,1,0:T(8,128)S(1)}, f32[4,3,4,6,1,128]{5,3,4,2,1,0:T(8,128)S(1)}, u32[]{:S(2)}, u32[]{:S(2)}) collective-permute-start(f32[4,3,4,6,1,128]{5,3,4,2,1,0:T(8,128)S(1)} %get-tuple-element.195), channel_id=1, source_target_pairs={{0,1},{1,2},{2,3},{3,4},{4,5},{5,6},{6,7},{7,0},{8,9},{9,10},{10,1... | collective-permute-start | bytes 442376 | tf_op jit(solution)/shard_map/ppermute | solution.py:17
  51.3 0.7 copy-start.10
  51.3 0.7 copy-start.11
  60.1 0.7 copy-start.8
  60.1 0.7 copy-start.9
  60.8 1.1 %copy-start.2 = (f32[4,4]{1,0:T(4,128)S(1)}, f32[4,4]{1,0:T(4,128)}, u32[]{:S(2)}) copy-start(f32[4,4]{1,0:T(4,128)} %constant.67.clone) | copy-start | bytes 196
  60.8 1.1 %copy-start.3 = (f32[4,4]{1,0:T(4,128)S(1)}, f32[4,4]{1,0:T(4,128)}, u32[]{:S(2)}) copy-start(f32[4,4]{1,0:T(4,128)} %constant.68.clone) | copy-start | bytes 196
  61.9 0.7 copy-start.5
  61.9 0.7 copy-start.6
  65.1 14.8 %collective-permute-start.11 = (f32[4,3,1,4,2,128]{5,3,4,2,1,0:T(4,128)S(1)}, f32[4,3,1,4,2,128]{5,3,4,2,1,0:T(4,128)S(1)}, u32[]{:S(2)}, u32[]{:S(2)}) collective-permute-start(f32[4,3,1,4,2,128]{5,3,4,2,1,0:T(4,128)S(1)} %get-tuple-element.220), channel_id=1, source_target_pairs={{0,448},{64,0},{128,64},{192,128},{256,192},{320,256},{384,320},{4... | collective-permute-start | bytes 147464 | tf_op jit(solution)/shard_map/ppermute | solution.py:29
  70.3 8.8 %collective-permute-start.10 = (f32[4,3,2,1,2,128]{5,3,4,2,1,0:T(1,128)S(1)}, f32[4,3,2,1,2,128]{5,3,4,2,1,0:T(1,128)S(1)}, u32[]{:S(2)}, u32[]{:S(2)}) collective-permute-start(f32[4,3,2,1,2,128]{5,3,4,2,1,0:T(1,128)S(1)} %fusion.17), channel_id=1, source_target_pairs={{0,56},{8,0},{16,8},{24,16},{32,24},{40,32},{48,40},{56,48},{1,57}... | collective-permute-start | bytes 73736 | tf_op jit(solution)/shard_map/ppermute | solution.py:29
  73.5 7.0 %collective-permute-start.9 = (f32[4,3,2,4,1,128]{5,3,4,2,1,0:T(4,128)S(1)}, f32[4,3,2,4,1,128]{5,3,4,2,1,0:T(4,128)S(1)}, u32[]{:S(2)}, u32[]{:S(2)}) collective-permute-start(f32[4,3,2,4,1,128]{5,3,4,2,1,0:T(4,128)S(1)} %get-tuple-element.222), channel_id=1, source_target_pairs={{0,7},{1,0},{2,1},{3,2},{4,3},{5,4},{6,5},{7,6},{8,15},{9,8},{10,9... | collective-permute-start | bytes 147464 | tf_op jit(solution)/shard_map/ppermute | solution.py:29
where the time goes:
time: 86.8 us; the launch traced here: 86.2 us
  starting transfers between devices  46 us (53%)
  other arithmetic  20.8 us (24%)
  local copies, waits for them, and re-layouts  11.3 us (13%)
  waiting for transfers between devices  6.39 us (7%)
  between operations  1.74 us (2%)
    ppermute x6, starting transfers between devices, shifted(): return lax.ppermute(value, axis, pairs)  22.7 us
    ppermute x3, starting transfers between devices, with_halo(): lax.ppermute(head, axis, [((i + 1) % count, i) for i in range(count)])  15.2 us
    ppermute x3, starting transfers between devices, with_halo(): lax.ppermute(tail, axis, [(i, (i + 1) % count) for i in range(count)])  8.06 us
    reduce_sum x24, other arithmetic, mix_apply(): return jnp.sum(factor * part[None], axis=1)  7.49 us
    unnamed x36, local copies, waits for them, and re-layouts  6.86 us
    ppermute x3, waiting for transfers between devices, with_halo(): lax.ppermute(tail, axis, [(i, (i + 1) % count) for i in range(count)])  5.14 us
    reduce_sum x7, other arithmetic, colour_times(): return jnp.sum(link[None] * part[:, None], axis=2)  3.16 us
    reduce_sum x2, other arithmetic, spin_outer(): return jnp.sum(left[:, :, None] * right[:, None, :], axis=0)  2.91 us
  transfers between devices with their start and end apart: 12, of which 3 were waited for; matrix products, arithmetic and copies ran while one was open for 18% of the time, Pallas kernels for 0%

commit v1 on v0

v1 whole, which is shorter than its diff:
```python
import jax
import jax.numpy as jnp
from jax import lax
from jax.experimental import pallas as pl
from jax.experimental.pallas import tpu as pltpu
from jax.sharding import PartitionSpec as P

KAPPA = 0.125
MESH = pl.DeviceIdType.MESH
X_DIR, Y_DIR, Z_DIR, T_DIR = 0, 1, 2, 3
AXES = {T_DIR: "ta", Z_DIR: "gz", Y_DIR: "gy"}
FACES = (T_DIR, Z_DIR, Y_DIR)
FACE_TILES = {T_DIR: 6, Z_DIR: 3, Y_DIR: 6}


def lane_roll(v, steps):
    return pltpu.roll(v.reshape(-1, 128), steps, 1).reshape(v.shape)


def row_roll(v, steps):
    if steps % 8 == 0:
        return v
    flat = v.reshape(-1, 8, 128)
    return jnp.stack([pltpu.roll(flat[i], steps % 8, 0) for i in range(flat.shape[0])]).reshape(v.shape)


def masks():
    lane = lax.broadcasted_iota(jnp.int32, (8, 128), 1)
    row = lax.broadcasted_iota(jnp.int32, (8, 128), 0)
    return {
        "low": lane < 64,
        "last_x": lane % 64 == 63,
        "first_x": lane % 64 == 0,
        "even": row % 2 == 0,
        "z_first": row < 2,
        "z_last": row >= 6,
        "row": row,
    }


def pick(mask, a, b):
    return jnp.where(jnp.broadcast_to(mask, a.shape), a, b)


def unpack(m, first, second):
    return (
        pick(m["low"], first, lane_roll(second, 64)),
        pick(m["low"], lane_roll(first, 64), second),
    )


def pack_first(m, re, im):
    return pick(m["low"], re, lane_roll(im, 64))


def pack_second(m, re, im):
    return pick(m["low"], lane_roll(re, 64), im)


def c_add(a, b):
    return (a[0] + b[0], a[1] + b[1])


def c_sub(a, b):
    return (a[0] - b[0], a[1] - b[1])


def add_i(a, b):
    return (a[0] - b[1], a[1] + b[0])


def sub_i(a, b):
    return (a[0] + b[1], a[1] - b[0])


def project(direction, sign, psi):
    u0, u1, l0, l1 = psi
    plus, minus = (c_add, c_sub) if sign < 0 else (c_sub, c_add)
    plus_i, minus_i = (add_i, sub_i) if sign < 0 else (sub_i, add_i)
    if direction == X_DIR:
        return [plus_i(u0, l1), plus_i(u1, l0)]
    if direction == Y_DIR:
        return [plus(u0, l1), minus(u1, l0)]
    if direction == Z_DIR:
        return [plus_i(u0, l0), minus_i(u1, l1)]
    return [minus(u0, l0), minus(u1, l1)]


def add_spins(direction, sign, total, half):
    h0, h1 = half
    plus, minus = (c_sub, c_add) if sign < 0 else (c_add, c_sub)
    plus_i, minus_i = (sub_i, add_i) if sign < 0 else (add_i, sub_i)
    t0, t1, t2, t3 = total
    upper = [c_add(t0, h0), c_add(t1, h1)]
    if direction == X_DIR:
        return upper + [plus_i(t2, h1), plus_i(t3, h0)]
    if direction == Y_DIR:
        return upper + [plus(t2, h1), minus(t3, h0)]
    if direction == Z_DIR:
        return upper + [plus_i(t2, h0), minus_i(t3, h1)]
    return upper + [plus(t2, h0), plus(t3, h1)]


def link_times(u, half):
    ur, ui = u
    out = []
    for hr, hi in half:
        re = im = None
        for b in range(3):
            cr, ci = ur[:, b], ui[:, b]
            r = cr * hr[b][None] - ci * hi[b][None]
            i = cr * hi[b][None] + ci * hr[b][None]
            re = r if re is None else re + r
            im = i if im is None else im + i
        out.append((re, im))
    return out


def adjoint_times(u, half):
    ur, ui = u
    out = []
    for hr, hi in half:
        re = im = None
        for b in range(3):
            cr, ci = ur[b], ui[b]
            r = cr * hr[b][None] + ci * hi[b][None]
            i = cr * hi[b][None] - ci * hr[b][None]
            re = r if re is None else re + r
            im = i if im is None else im + i
        out.append((re, im))
    return out


def outer(left, right):
    re = im = None
    for (lr, li), (rr, ri) in zip(left, right):
        r = lr[:, None] * rr[None] + li[:, None] * ri[None]
        i = li[:, None] * rr[None] - lr[:, None] * ri[None]
        re = r if re is None else re + r
        im = i if im is None else im + i
    return re, im


def shift_x(m, half, steps):
    def one(v):
        if steps > 0:
            return pick(m["last_x"], lane_roll(v, 63), lane_roll(v, 127))
        return pick(m["first_x"], lane_roll(v, 65), lane_roll(v, 1))

    return [(one(re), one(im)) for re, im in half]


def stage_face(m, direction, end, half, ref):
    if direction == T_DIR:
        for s, (re, im) in enumerate(half):
            ref[3 * s:3 * s + 3] = (pack_second if end else pack_first)(m, re, im)
    elif direction == Y_DIR:
        for s, (re, im) in enumerate(half):
            if end:
                tile = pick(m["even"], row_roll(re, -1), im)
            else:
                tile = pick(m["even"], re, row_roll(im, 1))
            ref[3 * s:3 * s + 3] = tile
    else:
        tiles = [part[c] for re, im in half for part in (re, im) for c in range(3)]
        for j in range(3):
            tile = row_roll(tiles[4 * j], 2 if end else 0)
            for k in range(1, 4):
                moved = row_roll(tiles[4 * j + k], 2 * k + (2 if end else 0))
                tile = pick(m["row"] < 2 * k, tile, moved)
            ref[j] = tile


def shift_face(m, direction, steps, half, ref, sign):
    out = []
    if direction == T_DIR:
        for s, (re, im) in enumerate(half):
            face = ref[3 * s:3 * s + 3] * sign
            if steps > 0:
                out.append((
                    lane_roll(pick(m["low"], face, re), 64),
                    pick(m["low"], lane_roll(im, 64), face),
                ))
            else:
                out.append((
                    pick(m["low"], face, lane_roll(re, 64)),
                    lane_roll(pick(m["low"], im, face), 64),
                ))
    elif direction == Y_DIR:
        for s, (re, im) in enumerate(half):
            face = ref[3 * s:3 * s + 3]
            if steps > 0:
                out.append((
                    pick(m["even"], row_roll(re, -1), row_roll(face, 1)),
                    pick(m["even"], row_roll(im, -1), face),
                ))
            else:
                out.append((
                    pick(m["even"], face, row_roll(re, 1)),
                    pick(m["even"], row_roll(face, -1), row_roll(im, 1)),
                ))
    else:
        n = 0
        for re, im in half:
            parts = []
            for part in (re, im):
                moved = []
                for c in range(3):
                    face = ref[n // 4]
                    k = n % 4
                    n += 1
                    if steps > 0:
                        moved.append(row_roll(pick(m["z_first"], row_roll(face, -2 * k), part[c]), -2))
                    else:
                        moved.append(row_roll(pick(m["z_last"], row_roll(face, 6 - 2 * k), part[c]), 2))
                parts.append(jnp.stack(moved))
            out.append(tuple(parts))
    return out


def kernel(
    x_hbm, u_hbm, y_hbm, f_hbm,
    x_buf, u_buf, y_buf, f_buf,
    st_t, st_z, st_y, rt_t, rt_z, rt_y,
    load_sem, send_sem, recv_sem, store_sem,
):
    send_buf = {T_DIR: st_t, Z_DIR: st_z, Y_DIR: st_y}
    recv_buf = {T_DIR: rt_t, Z_DIR: rt_z, Y_DIR: rt_y}
    x_load = pltpu.make_async_copy(x_hbm, x_buf, load_sem.at[4])
    x_load.start()
    u_load = {}
    for d in (T_DIR, Z_DIR, Y_DIR, X_DIR):
        u_load[d] = pltpu.make_async_copy(u_hbm.at[d], u_buf.at[d], load_sem.at[d])
        u_load[d].start()

    me = {d: lax.axis_index(AXES[d]) for d in FACES}
    size = {d: lax.axis_size(AXES[d]) for d in FACES}
    ahead = {d: lax.rem(me[d] + 1, size[d]) for d in FACES}
    behind = {d: lax.rem(me[d] + size[d] - 1, size[d]) for d in FACES}

    barrier = pltpu.get_barrier_semaphore()
    for d in FACES:
        for there in (ahead[d], behind[d]):
            pl.semaphore_signal(barrier, inc=1, device_id={AXES[d]: there}, device_id_type=MESH)

    def send(d, slot, there):
        n = 3 * (d - 1) + slot
        copy = pltpu.make_async_remote_copy(
            src_ref=send_buf[d].at[slot],
            dst_ref=recv_buf[d].at[slot],
            send_sem=send_sem.at[n],
            recv_sem=recv_sem.at[n],
            device_id={AXES[d]: there},
            device_id_type=MESH,
        )
        copy.start()
        return copy

    m = masks()
    last_t = jnp.where(me[T_DIR] == size[T_DIR] - 1, -1.0, 1.0).astype(jnp.float32)
    first_t = jnp.where(me[T_DIR] == 0, -1.0, 1.0).astype(jnp.float32)
    ahead_sign = {T_DIR: last_t, Z_DIR: None, Y_DIR: None}
    behind_sign = {T_DIR: first_t, Z_DIR: None, Y_DIR: None}

    x_load.wait()
    psi = [unpack(m, x_buf[3 * s:3 * s + 3, 0:8], x_buf[3 * s:3 * s + 3, 8:16]) for s in range(4)]
    minus = {}
    plus = {}
    for d in FACES:
        minus[d] = project(d, -1, psi)
        stage_face(m, d, 0, minus[d], send_buf[d].at[0])
    pl.semaphore_wait(barrier, 6)
    copies = [send(d, 0, behind[d]) for d in FACES]
    forward = dict(zip(FACES, copies))

    def links(d):
        first, second = unpack(m, u_buf[d, :, 0:8], u_buf[d, :, 8:16])
        return first.reshape(3, 3, 8, 128), second.reshape(3, 3, 8, 128)

    u = {}
    back = {}
    backward = {}
    for d in FACES:
        u_load[d].wait()
        u[d] = links(d)
        plus[d] = project(d, 1, psi)
        back[d] = adjoint_times(u[d], plus[d])
        stage_face(m, d, 1, back[d], send_buf[d].at[1])
        backward[d] = send(d, 1, ahead[d])

    zero = jnp.zeros((3, 8, 128), jnp.float32)
    hop = [(zero, zero)] * 4
    d = X_DIR
    u_load[d].wait()
    u[d] = links(d)
    plus[d] = project(d, 1, psi)
    minus[d] = project(d, -1, psi)
    moved = {}
    moved[d] = link_times(u[d], shift_x(m, minus[d], 1))
    hop = add_spins(d, -1, hop, moved[d])
    hop = add_spins(d, 1, hop, shift_x(m, adjoint_times(u[d], plus[d]), -1))
    for d in FACES:
        forward[d].wait_recv()
        there = shift_face(m, d, 1, minus[d], recv_buf[d].at[0], ahead_sign[d])
        moved[d] = link_times(u[d], there)
        hop = add_spins(d, -1, hop, moved[d])
    for d in FACES:
        backward[d].wait_recv()
        there = shift_face(m, d, -1, back[d], recv_buf[d].at[1], behind_sign[d])
        hop = add_spins(d, 1, hop, there)

    result = [
        (pr - KAPPA * hr, pi - KAPPA * hi) for (pr, pi), (hr, hi) in zip(psi, hop)
    ]
    later = {}
    upward = {}
    for d in FACES:
        later[d] = project(d, 1, result)
        stage_face(m, d, 0, later[d], send_buf[d].at[2])
        upward[d] = send(d, 2, behind[d])
    for s, (re, im) in enumerate(result):
        y_buf[3 * s:3 * s + 3, 0:8] = pack_first(m, re, im)
        y_buf[3 * s:3 * s + 3, 8:16] = pack_second(m, re, im)
    stores = [pltpu.make_async_copy(y_buf, y_hbm, store_sem.at[4])]
    stores[0].start()

    def finish(d, first, later_there):
        second = outer(link_times(u[d], later_there), plus[d])
        wr, wi = c_add(first, second)
        third = (wi[0, 0] + wi[1, 1] + wi[2, 2]) / 3.0
        for a in range(3):
            for b in range(a, 3):
                if a == b:
                    im = KAPPA * (wi[a, a] - third)
                    re = jnp.zeros_like(im)
                else:
                    re = (0.5 * KAPPA) * (wr[a, b] - wr[b, a])
                    im = (0.5 * KAPPA) * (wi[a, b] + wi[b, a])
                top = pack_first(m, re, im)
                bottom = pack_second(m, re, im)
                f_buf[d, 3 * a + b, 0:8] = top
                f_buf[d, 3 * a + b, 8:16] = bottom
                if a != b:
                    f_buf[d, 3 * b + a, 0:8] = pick(m["low"], -top, top)
                    f_buf[d, 3 * b + a, 8:16] = pick(m["low"], -bottom, bottom)
        store = pltpu.make_async_copy(f_buf.at[d], f_hbm.at[d], store_sem.at[d])
        store.start()
        stores.append(store)

    d = X_DIR
    finish(d, outer(moved[d], project(d, -1, result)), shift_x(m, project(d, 1, result), 1))
    first = {d: outer(moved[d], project(d, -1, result)) for d in FACES}
    for d in FACES:
        upward[d].wait_recv()
        finish(d, first[d], shift_face(m, d, 1, later[d], recv_buf[d].at[2], ahead_sign[d]))
    for d in FACES:
        forward[d].wait_send()
        backward[d].wait_send()
        upward[d].wait_send()
    for store in stores:
        store.wait()


def body(quark_field, gauge_links):
    x = quark_field.reshape(12, 16, 128)
    u = gauge_links.reshape(4, 9, 16, 128)
    faces = [pltpu.VMEM((3, FACE_TILES[d], 8, 128), jnp.float32) for d in FACES]
    y, f = pl.pallas_call(
        kernel,
        out_shape=(
            jax.ShapeDtypeStruct(x.shape, jnp.float32),
            jax.ShapeDtypeStruct(u.shape, jnp.float32),
        ),
        in_specs=[pl.BlockSpec(memory_space=pl.ANY)] * 2,
        out_specs=(pl.BlockSpec(memory_space=pl.ANY),) * 2,
        scratch_shapes=[
            pltpu.VMEM(x.shape, jnp.float32),
            pltpu.VMEM(u.shape, jnp.float32),
            pltpu.VMEM(x.shape, jnp.float32),
            pltpu.VMEM(u.shape, jnp.float32),
            *faces,
            *faces,
            pltpu.SemaphoreType.DMA((5,)),
            pltpu.SemaphoreType.DMA((9,)),
            pltpu.SemaphoreType.DMA((9,)),
            pltpu.SemaphoreType.DMA((5,)),
        ],
        compiler_params=pltpu.CompilerParams(collective_id=0, has_side_effects=True),
        cost_estimate=pl.CostEstimate(flops=6_000_000, bytes_accessed=800_000, transcendentals=0),
    )(x, u)
    return y.reshape(quark_field.shape), f.reshape(gauge_links.shape)


def solution(mesh):
    specs = (
        P(None, None, "ta", "gz", "gy", None),
        P(None, None, None, "ta", "gz", "gy", None),
    )
    return jax.shard_map(body, mesh=mesh, in_specs=specs, out_specs=specs, check_vma=False)
```

time: 86.8 us -> 26.3 us (0.30)
  starting transfers between devices: 46 us -> 0 us
  Pallas kernels: 0 us -> 22.2 us
  other arithmetic: 20.8 us -> 0 us
  local copies, waits for them, and re-layouts: 11.3 us -> 3.23 us
  waiting for transfers between devices: 6.39 us -> 0 us
  between operations: 1.74 us -> 0.64 us
    ppermute x12 -> x0, starting transfers between devices: 46 us -> none  [the longest x6 22.7 us: shifted(): return lax.ppermute(value, axis, pairs)]
    pallas_call x0 -> x1, Pallas kernels: none -> 22.2 us  [body(): pl.pallas_call(kernel, out_shape=(jax.ShapeDtypeStruct(x.shape, jnp.float...]
    reduce_sum x37 -> x0, other arithmetic: 14.7 us -> none  [the longest x24 7.49 us: mix_apply(): return jnp.sum(factor * part[None], axis=1)]
    ppermute x12 -> x0, waiting for transfers between devices: 6.39 us -> none  [the longest x3 5.14 us: with_halo(): lax.ppermute(tail, axis, [(i, (i + 1) % count) for i in range(count)])]
    unnamed x36 -> x2, local copies, waits for them, and re-layouts: 6.86 us -> 3.23 us
    slice x16 -> x0, local copies, waits for them, and re-layouts: 2.47 us -> none  [the longest x4 1.03 us: roll_cells(): return jnp.roll(shaped, -stride, axis=-1).reshape(merged.shape)]
    concatenate x12 -> x0, other arithmetic: 2.07 us -> none  [the longest x3 0.98 us: roll_cells(): return jnp.roll(shaped, -stride, axis=-1).reshape(merged.shape)]
    add x24 -> x0, other arithmetic: 1.11 us -> none  [the longest x8 0.69 us: spin_project(): part_imag + mix_apply(mix_real, part_imag) + mix_apply(mix_imag, part_real)]
  transfers between devices with their start and end apart: 12 -> 0, of which waited for: 3 -> 0; matrix products, arithmetic and copies ran while one was open for 18% -> 0% of each run, Pallas kernels for 0% -> 0%
where the time goes in v1:
time: 26.3 us; the launch traced here: 26 us
  Pallas kernels  22.2 us (84%)
  local copies, waits for them, and re-layouts  3.23 us (12%)
  between operations  0.64 us (2%)
    pallas_call x1, Pallas kernels, body(): pl.pallas_call(kernel, out_shape=(jax.ShapeDtypeStruct(x.shape, jnp.float...  22.2 us
    unnamed x2, local copies, waits for them, and re-layouts  3.23 us

profile of v1, /device:TPU:1, one launch (start us, length us, event | category | flops | bytes accessed | tf_op | source)
XLA Modules:
  0.0 26.0 jit_solution(17252815142632128308)
XLA Ops:
  0.6 22.2 %shard_map.41 = (f32[12,16,128]{2,1,0:T(8,128)}, f32[4,9,16,128]{3,2,1,0:T(8,128)}) custom-call(f32[12,16,128]{2,1,0:T(8,128)} %bitcast.7, f32[4,9,16,128]{3,2,1,0:T(8,128)} %bitcast.4), custom_call_target="tpu_custom_call" | custom-call | flops 6000000 | bytes 800000 | tf_op jit(solution)/shard_map/pallas_call | solution.py:368
  22.8 1.5 %copy.6 = f32[4,3,2,4,2,128]{5,4,3,2,1,0:T(2,128)} copy(f32[4,3,2,4,2,128]{5,4,3,2,1,0:T(2,128)} %bitcast.6) | data formatting | bytes 196608
  24.4 1.7 %copy.7 = f32[4,3,3,2,4,2,128]{6,5,4,3,2,1,0:T(2,128)} copy(f32[4,3,3,2,4,2,128]{6,5,4,3,2,1,0:T(2,128)} %bitcast.5) | data formatting | bytes 589824

commit v2 on v1

--- a/solution.py
+++ b/solution.py
@@ -219,29 +219,29 @@
 
 
 def kernel(
-    x_hbm, u_hbm, y_hbm, f_hbm,
-    x_buf, u_buf, y_buf, f_buf,
+    x_hbm, u_hbm, y_buf, f_buf,
+    x_buf, u_buf,
     st_t, st_z, st_y, rt_t, rt_z, rt_y,
-    load_sem, send_sem, recv_sem, store_sem,
+    load_sem, send_sem, recv_sem,
 ):
     send_buf = {T_DIR: st_t, Z_DIR: st_z, Y_DIR: st_y}
     recv_buf = {T_DIR: rt_t, Z_DIR: rt_z, Y_DIR: rt_y}
+    me = {d: lax.axis_index(AXES[d]) for d in FACES}
+    size = {d: lax.axis_size(AXES[d]) for d in FACES}
+    ahead = {d: lax.rem(me[d] + 1, size[d]) for d in FACES}
+    behind = {d: lax.rem(me[d] + size[d] - 1, size[d]) for d in FACES}
+
+    barrier = pltpu.get_barrier_semaphore()
+    for d in FACES:
+        for there in (ahead[d], behind[d]):
+            pl.semaphore_signal(barrier, inc=1, device_id={AXES[d]: there}, device_id_type=MESH)
+
     x_load = pltpu.make_async_copy(x_hbm, x_buf, load_sem.at[4])
     x_load.start()
     u_load = {}
     for d in (T_DIR, Z_DIR, Y_DIR, X_DIR):
         u_load[d] = pltpu.make_async_copy(u_hbm.at[d], u_buf.at[d], load_sem.at[d])
         u_load[d].start()
-
-    me = {d: lax.axis_index(AXES[d]) for d in FACES}
-    size = {d: lax.axis_size(AXES[d]) for d in FACES}
-    ahead = {d: lax.rem(me[d] + 1, size[d]) for d in FACES}
-    behind = {d: lax.rem(me[d] + size[d] - 1, size[d]) for d in FACES}
-
-    barrier = pltpu.get_barrier_semaphore()
-    for d in FACES:
-        for there in (ahead[d], behind[d]):
-            pl.semaphore_signal(barrier, inc=1, device_id={AXES[d]: there}, device_id_type=MESH)
 
     def send(d, slot, there):
         n = 3 * (d - 1) + slot
@@ -321,8 +321,6 @@
     for s, (re, im) in enumerate(result):
         y_buf[3 * s:3 * s + 3, 0:8] = pack_first(m, re, im)
         y_buf[3 * s:3 * s + 3, 8:16] = pack_second(m, re, im)
-    stores = [pltpu.make_async_copy(y_buf, y_hbm, store_sem.at[4])]
-    stores[0].start()
 
     def finish(d, first, later_there):
         second = outer(link_times(u[d], later_there), plus[d])
@@ -343,9 +341,6 @@
                 if a != b:
                     f_buf[d, 3 * b + a, 0:8] = pick(m["low"], -top, top)
                     f_buf[d, 3 * b + a, 8:16] = pick(m["low"], -bottom, bottom)
-        store = pltpu.make_async_copy(f_buf.at[d], f_hbm.at[d], store_sem.at[d])
-        store.start()
-        stores.append(store)
 
     d = X_DIR
     finish(d, outer(moved[d], project(d, -1, result)), shift_x(m, project(d, 1, result), 1))
@@ -357,8 +352,15 @@
         forward[d].wait_send()
         backward[d].wait_send()
         upward[d].wait_send()
-    for store in stores:
-        store.wait()
+
+
+def store_kernel(y_in, f_in, y_out, f_out, sems):
+    copies = [pltpu.make_async_copy(y_in, y_out, sems.at[4])]
+    copies += [pltpu.make_async_copy(f_in.at[d], f_out.at[d], sems.at[d]) for d in range(4)]
+    for copy in copies:
+        copy.start()
+    for copy in copies:
+        copy.wait()
 
 
 def body(quark_field, gauge_links):
@@ -367,15 +369,10 @@
     faces = [pltpu.VMEM((3, FACE_TILES[d], 8, 128), jnp.float32) for d in FACES]
     y, f = pl.pallas_call(
         kernel,
-        out_shape=(
-            jax.ShapeDtypeStruct(x.shape, jnp.float32),
-            jax.ShapeDtypeStruct(u.shape, jnp.float32),
-        ),
-        in_specs=[pl.BlockSpec(memory_space=pl.ANY)] * 2,
-        out_specs=(pl.BlockSpec(memory_space=pl.ANY),) * 2,
+        out_shape=(pltpu.VMEM(x.shape, jnp.float32), pltpu.VMEM(u.shape, jnp.float32)),
+        in_specs=[pl.BlockSpec(memory_space=pltpu.HBM)] * 2,
+        out_specs=(pl.BlockSpec(memory_space=pltpu.VMEM),) * 2,
         scratch_shapes=[
-            pltpu.VMEM(x.shape, jnp.float32),
-            pltpu.VMEM(u.shape, jnp.float32),
             pltpu.VMEM(x.shape, jnp.float32),
             pltpu.VMEM(u.shape, jnp.float32),
             *faces,
@@ -383,11 +380,22 @@
             pltpu.SemaphoreType.DMA((5,)),
             pltpu.SemaphoreType.DMA((9,)),
             pltpu.SemaphoreType.DMA((9,)),
-            pltpu.SemaphoreType.DMA((5,)),
         ],
-        compiler_params=pltpu.CompilerParams(collective_id=0, has_side_effects=True),
+        compiler_params=pltpu.CompilerParams(collective_id=0, has_side_effects=True, vmem_limit_bytes=16 * 1024 * 1024),
         cost_estimate=pl.CostEstimate(flops=6_000_000, bytes_accessed=800_000, transcendentals=0),
-    )(x, u)
+    )(pltpu.with_memory_space_constraint(x, pltpu.HBM), pltpu.with_memory_space_constraint(u, pltpu.HBM))
+    y, f = pl.pallas_call(
+        store_kernel,
+        out_shape=(
+            jax.ShapeDtypeStruct(x.shape, jnp.float32),
+            jax.ShapeDtypeStruct(u.shape, jnp.float32),
+        ),
+        in_specs=[pl.BlockSpec(memory_space=pltpu.VMEM)] * 2,
+        out_specs=(pl.BlockSpec(memory_space=pl.ANY),) * 2,
+        scratch_shapes=[pltpu.SemaphoreType.DMA((5,))],
+        compiler_params=pltpu.CompilerParams(vmem_limit_bytes=16 * 1024 * 1024),
+        cost_estimate=pl.CostEstimate(flops=0, bytes_accessed=800_000, transcendentals=0),
+    )(y, f)
     return y.reshape(quark_field.shape), f.reshape(gauge_links.shape)
 
 

time: 26.3 us -> 23.1 us (0.88)
  local copies, waits for them, and re-layouts: 3.23 us -> 0 us
    unnamed x2 -> x0, local copies, waits for them, and re-layouts: 3.23 us -> none
    pallas_call x1 -> x2, Pallas kernels: 22.2 us -> 22.3 us  [the longest x1 21.5 us: body(): pl.pallas_call(kernel, out_shape=(pltpu.VMEM(x.shape, jnp.float32), pltpu...]
where the time goes in v2:
time: 23.1 us; the launch traced here: 22.9 us
  Pallas kernels  22.3 us (97%)
  between operations  0.64 us (3%)
    pallas_call x1, Pallas kernels, body(): pl.pallas_call(kernel, out_shape=(pltpu.VMEM(x.shape, jnp.float32), pltpu...  21.5 us
    pallas_call x1, Pallas kernels, body(): pl.pallas_call(store_kernel, out_shape=(jax.ShapeDtypeStruct(x.shape, jnp...  0.78 us

profile of v2, /device:TPU:1, one launch (start us, length us, event | category | flops | bytes accessed | tf_op | source)
XLA Modules:
  0.0 22.9 jit_solution(8857340990321539923)
XLA Ops:
  0.6 21.5 %shard_map.41 = (f32[12,16,128]{2,1,0:T(8,128)S(1)}, f32[4,9,16,128]{3,2,1,0:T(8,128)S(1)}) custom-call(f32[12,16,128]{2,1,0:T(8,128)} %bitcast.5, f32[4,9,16,128]{3,2,1,0:T(8,128)} %bitcast.4), custom_call_target="tpu_custom_call" | custom-call | flops 6000000 | bytes 800000 | tf_op jit(solution)/shard_map/pallas_call | solution.py:370
  22.2 0.8 %shard_map.42 = (f32[12,16,128]{2,1,0:T(8,128)}, f32[4,9,16,128]{3,2,1,0:T(8,128)}) custom-call(f32[12,16,128]{2,1,0:T(8,128)S(1)} %get-tuple-element.6.y_in, f32[4,9,16,128]{3,2,1,0:T(8,128)S(1)} %get-tuple-element.7.f_in), custom_call_target="tpu_custom_call" | custom-call | bytes 800000 | tf_op jit(solution)/shard_map/pallas_call | solution.py:387

commit v3 on v2

--- a/solution.py
+++ b/solution.py
@@ -232,10 +232,15 @@
     behind = {d: lax.rem(me[d] + size[d] - 1, size[d]) for d in FACES}
 
     barrier = pltpu.get_barrier_semaphore()
-    for d in FACES:
-        for there in (ahead[d], behind[d]):
-            pl.semaphore_signal(barrier, inc=1, device_id={AXES[d]: there}, device_id_type=MESH)
-
+    is_first = {d: me[d] == 0 for d in FACES}
+    for d in FACES:
+        pl.semaphore_signal(barrier, inc=1, device_id={AXES[d]: behind[d]}, device_id_type=MESH)
+
+        @pl.when(me[d] != size[d] - 1)
+        def _(d=d):
+            pl.semaphore_signal(barrier, inc=1, device_id={AXES[d]: ahead[d]}, device_id_type=MESH)
+
+    arrivals = 6 - sum(is_first[d].astype(jnp.int32) for d in FACES)
     x_load = pltpu.make_async_copy(x_hbm, x_buf, load_sem.at[4])
     x_load.start()
     u_load = {}
@@ -243,9 +248,9 @@
         u_load[d] = pltpu.make_async_copy(u_hbm.at[d], u_buf.at[d], load_sem.at[d])
         u_load[d].start()
 
-    def send(d, slot, there):
+    def link(d, slot, there):
         n = 3 * (d - 1) + slot
-        copy = pltpu.make_async_remote_copy(
+        return pltpu.make_async_remote_copy(
             src_ref=send_buf[d].at[slot],
             dst_ref=recv_buf[d].at[slot],
             send_sem=send_sem.at[n],
@@ -253,8 +258,10 @@
             device_id={AXES[d]: there},
             device_id_type=MESH,
         )
-        copy.start()
-        return copy
+
+    forward = {d: link(d, 0, behind[d]) for d in FACES}
+    backward = {d: link(d, 1, ahead[d]) for d in FACES}
+    upward = {d: link(d, 2, behind[d]) for d in FACES}
 
     m = masks()
     last_t = jnp.where(me[T_DIR] == size[T_DIR] - 1, -1.0, 1.0).astype(jnp.float32)
@@ -269,9 +276,6 @@
     for d in FACES:
         minus[d] = project(d, -1, psi)
         stage_face(m, d, 0, minus[d], send_buf[d].at[0])
-    pl.semaphore_wait(barrier, 6)
-    copies = [send(d, 0, behind[d]) for d in FACES]
-    forward = dict(zip(FACES, copies))
 
     def links(d):
         first, second = unpack(m, u_buf[d, :, 0:8], u_buf[d, :, 8:16])
@@ -279,14 +283,18 @@
 
     u = {}
     back = {}
-    backward = {}
     for d in FACES:
         u_load[d].wait()
         u[d] = links(d)
         plus[d] = project(d, 1, psi)
         back[d] = adjoint_times(u[d], plus[d])
         stage_face(m, d, 1, back[d], send_buf[d].at[1])
-        backward[d] = send(d, 1, ahead[d])
+
+    pl.semaphore_wait(barrier, arrivals)
+    for d in FACES:
+        backward[d].start()
+    for d in FACES:
+        pl.when(jnp.logical_not(is_first[d]))(forward[d].start)
 
     zero = jnp.zeros((3, 8, 128), jnp.float32)
     hop = [(zero, zero)] * 4
@@ -299,25 +307,33 @@
     moved[d] = link_times(u[d], shift_x(m, minus[d], 1))
     hop = add_spins(d, -1, hop, moved[d])
     hop = add_spins(d, 1, hop, shift_x(m, adjoint_times(u[d], plus[d]), -1))
-    for d in FACES:
+
+    def take_backward(d, hop):
+        backward[d].wait_recv()
+        pl.when(is_first[d])(forward[d].start)
+        there = shift_face(m, d, -1, back[d], recv_buf[d].at[1], behind_sign[d])
+        return add_spins(d, 1, hop, there)
+
+    def take_forward(d, hop):
         forward[d].wait_recv()
         there = shift_face(m, d, 1, minus[d], recv_buf[d].at[0], ahead_sign[d])
         moved[d] = link_times(u[d], there)
-        hop = add_spins(d, -1, hop, moved[d])
-    for d in FACES:
-        backward[d].wait_recv()
-        there = shift_face(m, d, -1, back[d], recv_buf[d].at[1], behind_sign[d])
-        hop = add_spins(d, 1, hop, there)
+        return add_spins(d, -1, hop, moved[d])
+
+    for d in (Z_DIR, T_DIR):
+        hop = take_backward(d, hop)
+    for d in (Z_DIR, T_DIR, Y_DIR):
+        hop = take_forward(d, hop)
+    hop = take_backward(Y_DIR, hop)
 
     result = [
         (pr - KAPPA * hr, pi - KAPPA * hi) for (pr, pi), (hr, hi) in zip(psi, hop)
     ]
     later = {}
-    upward = {}
-    for d in FACES:
+    for d in (Z_DIR, T_DIR, Y_DIR):
         later[d] = project(d, 1, result)
         stage_face(m, d, 0, later[d], send_buf[d].at[2])
-        upward[d] = send(d, 2, behind[d])
+        upward[d].start()
     for s, (re, im) in enumerate(result):
         y_buf[3 * s:3 * s + 3, 0:8] = pack_first(m, re, im)
         y_buf[3 * s:3 * s + 3, 8:16] = pack_second(m, re, im)
@@ -345,7 +361,7 @@
     d = X_DIR
     finish(d, outer(moved[d], project(d, -1, result)), shift_x(m, project(d, 1, result), 1))
     first = {d: outer(moved[d], project(d, -1, result)) for d in FACES}
-    for d in FACES:
+    for d in (Y_DIR, T_DIR, Z_DIR):
         upward[d].wait_recv()
         finish(d, first[d], shift_face(m, d, 1, later[d], recv_buf[d].at[2], ahead_sign[d]))
     for d in FACES:

time: 23.1 us -> 20.5 us (0.89)
  the two profiles are of different devices: /device:TPU:1 before, /device:TPU:23 now
where the time goes in v3:
time: 20.5 us; the launch traced here: 20.3 us
  Pallas kernels  19.7 us (96%)
  between operations  0.64 us (3%)
    pallas_call x1, Pallas kernels, body(): pl.pallas_call(kernel, out_shape=(pltpu.VMEM(x.shape, jnp.float32), pltpu...  18.9 us
    pallas_call x1, Pallas kernels, body(): pl.pallas_call(store_kernel, out_shape=(jax.ShapeDtypeStruct(x.shape, jnp...  0.78 us

profile of v3, /device:TPU:23, one launch (start us, length us, event | category | flops | bytes accessed | tf_op | source)
XLA Modules:
  0.0 20.3 jit_solution(18091653690218059106)
XLA Ops:
  0.6 18.9 %shard_map.41 = (f32[12,16,128]{2,1,0:T(8,128)S(1)}, f32[4,9,16,128]{3,2,1,0:T(8,128)S(1)}) custom-call(f32[12,16,128]{2,1,0:T(8,128)} %bitcast.5, f32[4,9,16,128]{3,2,1,0:T(8,128)} %bitcast.4), custom_call_target="tpu_custom_call" | custom-call | flops 6000000 | bytes 800000 | tf_op jit(solution)/shard_map/pallas_call | solution.py:386
  19.5 0.8 %shard_map.42 = (f32[12,16,128]{2,1,0:T(8,128)}, f32[4,9,16,128]{3,2,1,0:T(8,128)}) custom-call(f32[12,16,128]{2,1,0:T(8,128)S(1)} %get-tuple-element.6.y_in, f32[4,9,16,128]{3,2,1,0:T(8,128)S(1)} %get-tuple-element.7.f_in), custom_call_target="tpu_custom_call" | custom-call | bytes 800000 | tf_op jit(solution)/shard_map/pallas_call | solution.py:403

commit v4 on v3

--- a/solution.py
+++ b/solution.py
@@ -1,3 +1,5 @@
+import functools
+
 import jax
 import jax.numpy as jnp
 from jax import lax
@@ -24,7 +26,7 @@
     return jnp.stack([pltpu.roll(flat[i], steps % 8, 0) for i in range(flat.shape[0])]).reshape(v.shape)
 
 
-def masks():
+def masks(at_start):
     lane = lax.broadcasted_iota(jnp.int32, (8, 128), 1)
     row = lax.broadcasted_iota(jnp.int32, (8, 128), 0)
     return {
@@ -35,6 +37,10 @@
         "z_first": row < 2,
         "z_last": row >= 6,
         "row": row,
+        "halo_now": row % 2 + at_start == 0,
+        "halo_late": row % 2 + (1 - at_start) == 0,
+        "edge_t": (row % 2 + (1 - at_start) == 0) & (lane >= 64),
+        "edge_z": row + 8 * (1 - at_start) == 6,
     }
 
 
@@ -218,11 +224,34 @@
     return out
 
 
+def only(mask, v):
+    return pick(mask, v, jnp.zeros_like(v))
+
+
+def local_y(m, half):
+    return [tuple(pick(m["even"], jnp.zeros_like(v), row_roll(v, 1)) for v in parts) for parts in half]
+
+
+def face_y(mask, ref, steps=0):
+    out = []
+    for s in range(2):
+        face = ref[3 * s:3 * s + 3]
+        if steps:
+            face = lane_roll(face, steps)
+        out.append((only(mask, face), only(mask, row_roll(face, -1))))
+    return out
+
+
+def edge_term(direction, half):
+    h0, h1 = half
+    return project(direction, 1, [h0, h1, h1, (-h0[0], -h0[1])])
+
+
 def kernel(
     x_hbm, u_hbm, y_buf, f_buf,
     x_buf, u_buf,
-    st_t, st_z, st_y, rt_t, rt_z, rt_y,
-    load_sem, send_sem, recv_sem,
+    st_t, st_z, st_y, rt_t, rt_z, rt_y, y_now, edge_t, edge_z,
+    load_sem, send_sem, recv_sem, here_sem,
 ):
     send_buf = {T_DIR: st_t, Z_DIR: st_z, Y_DIR: st_y}
     recv_buf = {T_DIR: rt_t, Z_DIR: rt_z, Y_DIR: rt_y}
@@ -240,7 +269,15 @@
         def _(d=d):
             pl.semaphore_signal(barrier, inc=1, device_id={AXES[d]: ahead[d]}, device_id_type=MESH)
 
-    arrivals = 6 - sum(is_first[d].astype(jnp.int32) for d in FACES)
+    is_last_y = me[Y_DIR] == size[Y_DIR] - 1
+
+    @pl.when(is_first[Y_DIR])
+    def _():
+        for d in (T_DIR, Z_DIR):
+            there = {AXES[d]: ahead[d], AXES[Y_DIR]: behind[Y_DIR]}
+            pl.semaphore_signal(barrier, inc=1, device_id=there, device_id_type=MESH)
+
+    arrivals = 6 - sum(is_first[d].astype(jnp.int32) for d in FACES) + 2 * is_last_y.astype(jnp.int32)
     x_load = pltpu.make_async_copy(x_hbm, x_buf, load_sem.at[4])
     x_load.start()
     u_load = {}
@@ -263,7 +300,35 @@
     backward = {d: link(d, 1, ahead[d]) for d in FACES}
     upward = {d: link(d, 2, behind[d]) for d in FACES}
 
-    m = masks()
+    def edge_link(n, d, src, dst):
+        return pltpu.make_async_remote_copy(
+            src_ref=src,
+            dst_ref=dst,
+            send_sem=send_sem.at[n],
+            recv_sem=recv_sem.at[n],
+            device_id={AXES[d]: behind[d], AXES[Y_DIR]: ahead[Y_DIR]},
+            device_id_type=MESH,
+        )
+
+    edges = {
+        T_DIR: edge_link(9, T_DIR, st_y.at[1], edge_t),
+        Z_DIR: edge_link(10, Z_DIR, st_y.at[1, :, 0:2], edge_z.at[:, 6:8]),
+    }
+
+    here = {T_DIR: here_sem.at[0], Z_DIR: here_sem.at[1]}
+
+    def say_here():
+        for d in (T_DIR, Z_DIR):
+
+            @pl.when(me[d] == size[d] - 1)
+            def _(d=d):
+                pl.semaphore_signal(here[d], inc=1, device_id={AXES[d]: ahead[d]}, device_id_type=MESH)
+
+    def greeted(d):
+        pl.semaphore_wait(here[d], 1)
+        forward[d].start()
+
+    m = masks(is_first[Y_DIR].astype(jnp.int32))
     last_t = jnp.where(me[T_DIR] == size[T_DIR] - 1, -1.0, 1.0).astype(jnp.float32)
     first_t = jnp.where(me[T_DIR] == 0, -1.0, 1.0).astype(jnp.float32)
     ahead_sign = {T_DIR: last_t, Z_DIR: None, Y_DIR: None}
@@ -291,10 +356,20 @@
         stage_face(m, d, 1, back[d], send_buf[d].at[1])
 
     pl.semaphore_wait(barrier, arrivals)
-    for d in FACES:
+    backward[Y_DIR].start()
+
+    @pl.when(is_last_y)
+    def _():
+        edges[T_DIR].start()
+        edges[Z_DIR].start()
+
+    say_here()
+    for d in (T_DIR, Z_DIR):
         backward[d].start()
     for d in FACES:
         pl.when(jnp.logical_not(is_first[d]))(forward[d].start)
+    for d in (T_DIR, Z_DIR):
+        pl.when(is_first[d])(functools.partial(greeted, d))
 
     zero = jnp.zeros((3, 8, 128), jnp.float32)
     hop = [(zero, zero)] * 4
@@ -310,7 +385,6 @@
 
     def take_backward(d, hop):
         backward[d].wait_recv()
-        pl.when(is_first[d])(forward[d].start)
         there = shift_face(m, d, -1, back[d], recv_buf[d].at[1], behind_sign[d])
         return add_spins(d, 1, hop, there)
 
@@ -324,16 +398,34 @@
         hop = take_backward(d, hop)
     for d in (Z_DIR, T_DIR, Y_DIR):
         hop = take_forward(d, hop)
-    hop = take_backward(Y_DIR, hop)
-
-    result = [
+    hop = add_spins(Y_DIR, 1, hop, local_y(m, back[Y_DIR]))
+
+    @pl.when(jnp.logical_not(is_first[Y_DIR]))
+    def _():
+        backward[Y_DIR].wait_recv()
+        y_now[...] = rt_y[1]
+
+    hop = add_spins(Y_DIR, 1, hop, face_y(m["halo_now"], y_now))
+    early = [
         (pr - KAPPA * hr, pi - KAPPA * hi) for (pr, pi), (hr, hi) in zip(psi, hop)
     ]
-    later = {}
-    for d in (Z_DIR, T_DIR, Y_DIR):
-        later[d] = project(d, 1, result)
-        stage_face(m, d, 0, later[d], send_buf[d].at[2])
+    for d in (Z_DIR, T_DIR):
+        stage_face(m, d, 0, project(d, 1, early), send_buf[d].at[2])
         upward[d].start()
+
+    @pl.when(is_first[Y_DIR])
+    def _():
+        backward[Y_DIR].wait_recv()
+        forward[Y_DIR].start()
+
+    zero_spins = [(zero, zero)] * 4
+    missing = add_spins(Y_DIR, 1, zero_spins, face_y(m["halo_late"], rt_y.at[1]))
+    result = [
+        (er - KAPPA * lr, ei - KAPPA * li) for (er, ei), (lr, li) in zip(early, missing)
+    ]
+    later = {d: project(d, 1, result) for d in FACES}
+    stage_face(m, Y_DIR, 0, later[Y_DIR], send_buf[Y_DIR].at[2])
+    upward[Y_DIR].start()
     for s, (re, im) in enumerate(result):
         y_buf[3 * s:3 * s + 3, 0:8] = pack_first(m, re, im)
         y_buf[3 * s:3 * s + 3, 8:16] = pack_second(m, re, im)
@@ -361,13 +453,31 @@
     d = X_DIR
     finish(d, outer(moved[d], project(d, -1, result)), shift_x(m, project(d, 1, result), 1))
     first = {d: outer(moved[d], project(d, -1, result)) for d in FACES}
-    for d in (Y_DIR, T_DIR, Z_DIR):
+    upward[Y_DIR].wait_recv()
+    finish(Y_DIR, first[Y_DIR], shift_face(m, Y_DIR, 1, later[Y_DIR], recv_buf[Y_DIR].at[2], None))
+    edge_half = {
+        T_DIR: lambda: face_y(m["edge_t"], edge_t, 64),
+        Z_DIR: lambda: face_y(m["edge_z"], edge_z),
+    }
+    for d in (T_DIR, Z_DIR):
         upward[d].wait_recv()
-        finish(d, first[d], shift_face(m, d, 1, later[d], recv_buf[d].at[2], ahead_sign[d]))
+        there = shift_face(m, d, 1, later[d], recv_buf[d].at[2], ahead_sign[d])
+        pl.when(is_first[Y_DIR])(edges[d].wait_recv)
+        scale = KAPPA * last_t if d == T_DIR else KAPPA
+        extra = edge_term(d, edge_half[d]())
+        there = [
+            (tr - scale * er, ti - scale * ei) for (tr, ti), (er, ei) in zip(there, extra)
+        ]
+        finish(d, first[d], there)
     for d in FACES:
         forward[d].wait_send()
         backward[d].wait_send()
         upward[d].wait_send()
+
+    @pl.when(is_last_y)
+    def _():
+        edges[T_DIR].wait_send()
+        edges[Z_DIR].wait_send()
 
 
 def store_kernel(y_in, f_in, y_out, f_out, sems):
@@ -393,9 +503,13 @@
             pltpu.VMEM(u.shape, jnp.float32),
             *faces,
             *faces,
+            pltpu.VMEM((6, 8, 128), jnp.float32),
+            pltpu.VMEM((6, 8, 128), jnp.float32),
+            pltpu.VMEM((6, 8, 128), jnp.float32),
             pltpu.SemaphoreType.DMA((5,)),
-            pltpu.SemaphoreType.DMA((9,)),
-            pltpu.SemaphoreType.DMA((9,)),
+            pltpu.SemaphoreType.DMA((11,)),
+            pltpu.SemaphoreType.DMA((11,)),
+            pltpu.SemaphoreType.REGULAR((2,)),
         ],
         compiler_params=pltpu.CompilerParams(collective_id=0, has_side_effects=True, vmem_limit_bytes=16 * 1024 * 1024),
         cost_estimate=pl.CostEstimate(flops=6_000_000, bytes_accessed=800_000, transcendentals=0),

time: 20.5 us -> 18.3 us (0.89)
  the two profiles are of different devices: /device:TPU:23 before, /device:TPU:6 now
where the time goes in v4:
time: 18.3 us; the launch traced here: 18.1 us
  Pallas kernels  17.5 us (96%)
  between operations  0.64 us (3%)
    pallas_call x1, Pallas kernels, body(): pl.pallas_call(kernel, out_shape=(pltpu.VMEM(x.shape, jnp.float32), pltpu...  16.7 us
    pallas_call x1, Pallas kernels, body(): pl.pallas_call(store_kernel, out_shape=(jax.ShapeDtypeStruct(x.shape, jnp...  0.78 us

profile of v4, /device:TPU:6, one launch (start us, length us, event | category | flops | bytes accessed | tf_op | source)
XLA Modules:
  0.0 18.1 jit_solution(7876649893478565842)
XLA Ops:
  0.6 16.7 %shard_map.41 = (f32[12,16,128]{2,1,0:T(8,128)S(1)}, f32[4,9,16,128]{3,2,1,0:T(8,128)S(1)}) custom-call(f32[12,16,128]{2,1,0:T(8,128)} %bitcast.5, f32[4,9,16,128]{3,2,1,0:T(8,128)} %bitcast.4), custom_call_target="tpu_custom_call" | custom-call | flops 6000000 | bytes 800000 | tf_op jit(solution)/shard_map/pallas_call | solution.py:496
  17.3 0.8 %shard_map.42 = (f32[12,16,128]{2,1,0:T(8,128)}, f32[4,9,16,128]{3,2,1,0:T(8,128)}) custom-call(f32[12,16,128]{2,1,0:T(8,128)S(1)} %get-tuple-element.6.y_in, f32[4,9,16,128]{3,2,1,0:T(8,128)S(1)} %get-tuple-element.7.f_in), custom_call_target="tpu_custom_call" | custom-call | bytes 800000 | tf_op jit(solution)/shard_map/pallas_call | solution.py:517

commit v5 on v4

--- a/solution.py
+++ b/solution.py
@@ -26,7 +26,7 @@
     return jnp.stack([pltpu.roll(flat[i], steps % 8, 0) for i in range(flat.shape[0])]).reshape(v.shape)
 
 
-def masks(at_start):
+def masks(at_start, at_end):
     lane = lax.broadcasted_iota(jnp.int32, (8, 128), 1)
     row = lax.broadcasted_iota(jnp.int32, (8, 128), 0)
     return {
@@ -39,6 +39,7 @@
         "row": row,
         "halo_now": row % 2 + at_start == 0,
         "halo_late": row % 2 + (1 - at_start) == 0,
+        "own_y": row % 2 * at_end == 1,
         "edge_t": (row % 2 + (1 - at_start) == 0) & (lane >= 64),
         "edge_z": row + 8 * (1 - at_start) == 6,
     }
@@ -232,14 +233,12 @@
     return [tuple(pick(m["even"], jnp.zeros_like(v), row_roll(v, 1)) for v in parts) for parts in half]
 
 
-def face_y(mask, ref, steps=0):
-    out = []
-    for s in range(2):
-        face = ref[3 * s:3 * s + 3]
-        if steps:
-            face = lane_roll(face, steps)
-        out.append((only(mask, face), only(mask, row_roll(face, -1))))
-    return out
+def face_y(mask, faces):
+    return [(only(mask, face), only(mask, row_roll(face, -1))) for face in faces]
+
+
+def both_spins(ref):
+    return [ref[0:3], ref[3:6]]
 
 
 def edge_term(direction, half):
@@ -250,11 +249,15 @@
 def kernel(
     x_hbm, u_hbm, y_buf, f_buf,
     x_buf, u_buf,
-    st_t, st_z, st_y, rt_t, rt_z, rt_y, y_now, edge_t, edge_z,
+    st_t, st_z, st_y, rt_t, rt_z, rt_y, y_now, edge_out, edge_t, edge_z,
     load_sem, send_sem, recv_sem, here_sem,
 ):
     send_buf = {T_DIR: st_t, Z_DIR: st_z, Y_DIR: st_y}
     recv_buf = {T_DIR: rt_t, Z_DIR: rt_z, Y_DIR: rt_y}
+    x_load = pltpu.make_async_copy(x_hbm, x_buf, load_sem.at[4])
+    u_load = {d: pltpu.make_async_copy(u_hbm.at[d], u_buf.at[d], load_sem.at[d]) for d in range(4)}
+    x_load.start()
+    u_load[Y_DIR].start()
     me = {d: lax.axis_index(AXES[d]) for d in FACES}
     size = {d: lax.axis_size(AXES[d]) for d in FACES}
     ahead = {d: lax.rem(me[d] + 1, size[d]) for d in FACES}
@@ -262,27 +265,25 @@
 
     barrier = pltpu.get_barrier_semaphore()
     is_first = {d: me[d] == 0 for d in FACES}
+    is_last = {d: me[d] == size[d] - 1 for d in FACES}
+    is_last_y = is_last[Y_DIR]
+
+    def greet(where):
+        pl.semaphore_signal(barrier, inc=1, device_id=where, device_id_type=MESH)
+
+    for d in (T_DIR, Z_DIR):
+        greet({AXES[d]: behind[d]})
     for d in FACES:
-        pl.semaphore_signal(barrier, inc=1, device_id={AXES[d]: behind[d]}, device_id_type=MESH)
-
-        @pl.when(me[d] != size[d] - 1)
-        def _(d=d):
-            pl.semaphore_signal(barrier, inc=1, device_id={AXES[d]: ahead[d]}, device_id_type=MESH)
-
-    is_last_y = me[Y_DIR] == size[Y_DIR] - 1
+        pl.when(jnp.logical_not(is_last[d]))(functools.partial(greet, {AXES[d]: ahead[d]}))
 
     @pl.when(is_first[Y_DIR])
     def _():
+        greet({AXES[Y_DIR]: behind[Y_DIR]})
         for d in (T_DIR, Z_DIR):
-            there = {AXES[d]: ahead[d], AXES[Y_DIR]: behind[Y_DIR]}
-            pl.semaphore_signal(barrier, inc=1, device_id=there, device_id_type=MESH)
-
-    arrivals = 6 - sum(is_first[d].astype(jnp.int32) for d in FACES) + 2 * is_last_y.astype(jnp.int32)
-    x_load = pltpu.make_async_copy(x_hbm, x_buf, load_sem.at[4])
-    x_load.start()
-    u_load = {}
-    for d in (T_DIR, Z_DIR, Y_DIR, X_DIR):
-        u_load[d] = pltpu.make_async_copy(u_hbm.at[d], u_buf.at[d], load_sem.at[d])
+            greet({AXES[d]: ahead[d], AXES[Y_DIR]: behind[Y_DIR]})
+
+    arrivals = 5 - sum(is_first[d].astype(jnp.int32) for d in FACES) + 3 * is_last_y.astype(jnp.int32)
+    for d in (T_DIR, Z_DIR, X_DIR):
         u_load[d].start()
 
     def link(d, slot, there):
@@ -311,24 +312,27 @@
         )
 
     edges = {
-        T_DIR: edge_link(9, T_DIR, st_y.at[1], edge_t),
+        T_DIR: edge_link(9, T_DIR, edge_out, edge_t),
         Z_DIR: edge_link(10, Z_DIR, st_y.at[1, :, 0:2], edge_z.at[:, 6:8]),
     }
 
-    here = {T_DIR: here_sem.at[0], Z_DIR: here_sem.at[1]}
+    here = {d: here_sem.at[d - 1] for d in FACES}
+    here_ahead = here_sem.at[3]
 
     def say_here():
-        for d in (T_DIR, Z_DIR):
-
-            @pl.when(me[d] == size[d] - 1)
-            def _(d=d):
-                pl.semaphore_signal(here[d], inc=1, device_id={AXES[d]: ahead[d]}, device_id_type=MESH)
+        def say(sem, there):
+            pl.semaphore_signal(sem, inc=1, device_id=there, device_id_type=MESH)
+
+        for d in FACES:
+            pl.when(is_last[d])(functools.partial(say, here[d], {AXES[d]: ahead[d]}))
+        there = {AXES[Y_DIR]: behind[Y_DIR]}
+        pl.when(jnp.logical_not(is_first[Y_DIR]))(functools.partial(say, here_ahead, there))
 
     def greeted(d):
         pl.semaphore_wait(here[d], 1)
         forward[d].start()
 
-    m = masks(is_first[Y_DIR].astype(jnp.int32))
+    m = masks(is_first[Y_DIR].astype(jnp.int32), is_last_y.astype(jnp.int32))
     last_t = jnp.where(me[T_DIR] == size[T_DIR] - 1, -1.0, 1.0).astype(jnp.float32)
     first_t = jnp.where(me[T_DIR] == 0, -1.0, 1.0).astype(jnp.float32)
     ahead_sign = {T_DIR: last_t, Z_DIR: None, Y_DIR: None}
@@ -338,38 +342,53 @@
     psi = [unpack(m, x_buf[3 * s:3 * s + 3, 0:8], x_buf[3 * s:3 * s + 3, 8:16]) for s in range(4)]
     minus = {}
     plus = {}
-    for d in FACES:
-        minus[d] = project(d, -1, psi)
-        stage_face(m, d, 0, minus[d], send_buf[d].at[0])
+    u = {}
+    back = {}
 
     def links(d):
         first, second = unpack(m, u_buf[d, :, 0:8], u_buf[d, :, 8:16])
         return first.reshape(3, 3, 8, 128), second.reshape(3, 3, 8, 128)
 
-    u = {}
-    back = {}
-    for d in FACES:
+    def prepare_backward(d):
         u_load[d].wait()
         u[d] = links(d)
         plus[d] = project(d, 1, psi)
         back[d] = adjoint_times(u[d], plus[d])
         stage_face(m, d, 1, back[d], send_buf[d].at[1])
 
-    pl.semaphore_wait(barrier, arrivals)
-    backward[Y_DIR].start()
+    prepare_backward(Y_DIR)
 
     @pl.when(is_last_y)
     def _():
+        edge_out[...] = pick(m["low"], st_y[1, 0:3], lane_roll(st_y[1, 3:6], 64))
+        pl.semaphore_wait(barrier, arrivals)
+        edges[Z_DIR].start()
         edges[T_DIR].start()
-        edges[Z_DIR].start()
-
-    say_here()
+        backward[Y_DIR].start()
+        say_here()
+
+    for d in FACES:
+        minus[d] = project(d, -1, psi)
+        stage_face(m, d, 0, minus[d], send_buf[d].at[0])
+    for d in (T_DIR, Z_DIR):
+        prepare_backward(d)
+
+    @pl.when(jnp.logical_not(is_last_y))
+    def _():
+        pl.semaphore_wait(barrier, arrivals)
+        say_here()
+
     for d in (T_DIR, Z_DIR):
         backward[d].start()
     for d in FACES:
         pl.when(jnp.logical_not(is_first[d]))(forward[d].start)
     for d in (T_DIR, Z_DIR):
         pl.when(is_first[d])(functools.partial(greeted, d))
+
+    @pl.when(jnp.logical_not(is_last_y))
+    def _():
+        pl.semaphore_wait(here_ahead, 1)
+        backward[Y_DIR].start()
 
     zero = jnp.zeros((3, 8, 128), jnp.float32)
     hop = [(zero, zero)] * 4
@@ -394,10 +413,12 @@
         moved[d] = link_times(u[d], there)
         return add_spins(d, -1, hop, moved[d])
 
-    for d in (Z_DIR, T_DIR):
-        hop = take_backward(d, hop)
-    for d in (Z_DIR, T_DIR, Y_DIR):
-        hop = take_forward(d, hop)
+    def wilson(hop):
+        return [(pr - KAPPA * hr, pi - KAPPA * hi) for (pr, pi), (hr, hi) in zip(psi, hop)]
+
+    hop = take_backward(Z_DIR, hop)
+    hop = take_forward(Z_DIR, hop)
+    hop = take_forward(Y_DIR, hop)
     hop = add_spins(Y_DIR, 1, hop, local_y(m, back[Y_DIR]))
 
     @pl.when(jnp.logical_not(is_first[Y_DIR]))
@@ -405,27 +426,32 @@
         backward[Y_DIR].wait_recv()
         y_now[...] = rt_y[1]
 
-    hop = add_spins(Y_DIR, 1, hop, face_y(m["halo_now"], y_now))
-    early = [
-        (pr - KAPPA * hr, pi - KAPPA * hi) for (pr, pi), (hr, hi) in zip(psi, hop)
-    ]
-    for d in (Z_DIR, T_DIR):
+    hop = add_spins(Y_DIR, 1, hop, face_y(m["halo_now"], both_spins(y_now)))
+
+    inner = [tuple(lane_roll(v, 64) for v in parts) for parts in minus[T_DIR]]
+    inner = add_spins(T_DIR, -1, hop, link_times(u[T_DIR], inner))
+    stage_face(m, T_DIR, 0, project(T_DIR, 1, wilson(inner)), send_buf[T_DIR].at[2])
+    upward[T_DIR].start()
+    hop = take_backward(T_DIR, hop)
+    hop = take_forward(T_DIR, hop)
+    early = wilson(hop)
+    for d in (Z_DIR, Y_DIR):
         stage_face(m, d, 0, project(d, 1, early), send_buf[d].at[2])
-        upward[d].start()
+    upward[Z_DIR].start()
+    pl.when(jnp.logical_not(is_first[Y_DIR]))(upward[Y_DIR].start)
 
     @pl.when(is_first[Y_DIR])
     def _():
+        greeted(Y_DIR)
+        upward[Y_DIR].start()
         backward[Y_DIR].wait_recv()
-        forward[Y_DIR].start()
-
-    zero_spins = [(zero, zero)] * 4
-    missing = add_spins(Y_DIR, 1, zero_spins, face_y(m["halo_late"], rt_y.at[1]))
+
+    late = face_y(m["halo_late"], both_spins(rt_y.at[1]))
+    missing = add_spins(Y_DIR, 1, [(zero, zero)] * 4, late)
     result = [
         (er - KAPPA * lr, ei - KAPPA * li) for (er, ei), (lr, li) in zip(early, missing)
     ]
     later = {d: project(d, 1, result) for d in FACES}
-    stage_face(m, Y_DIR, 0, later[Y_DIR], send_buf[Y_DIR].at[2])
-    upward[Y_DIR].start()
     for s, (re, im) in enumerate(result):
         y_buf[3 * s:3 * s + 3, 0:8] = pack_first(m, re, im)
         y_buf[3 * s:3 * s + 3, 8:16] = pack_second(m, re, im)
@@ -454,14 +480,24 @@
     finish(d, outer(moved[d], project(d, -1, result)), shift_x(m, project(d, 1, result), 1))
     first = {d: outer(moved[d], project(d, -1, result)) for d in FACES}
     upward[Y_DIR].wait_recv()
-    finish(Y_DIR, first[Y_DIR], shift_face(m, Y_DIR, 1, later[Y_DIR], recv_buf[Y_DIR].at[2], None))
+    there = shift_face(m, Y_DIR, 1, later[Y_DIR], recv_buf[Y_DIR].at[2], None)
+    there = [
+        (tr - 2 * KAPPA * only(m["own_y"], br), ti - 2 * KAPPA * only(m["own_y"], bi))
+        for (tr, ti), (br, bi) in zip(there, back[Y_DIR])
+    ]
+    finish(Y_DIR, first[Y_DIR], there)
     edge_half = {
-        T_DIR: lambda: face_y(m["edge_t"], edge_t, 64),
-        Z_DIR: lambda: face_y(m["edge_z"], edge_z),
+        T_DIR: lambda: face_y(m["edge_t"], [lane_roll(edge_t[...], 64), edge_t[...]]),
+        Z_DIR: lambda: face_y(m["edge_z"], both_spins(edge_z)),
     }
     for d in (T_DIR, Z_DIR):
         upward[d].wait_recv()
         there = shift_face(m, d, 1, later[d], recv_buf[d].at[2], ahead_sign[d])
+        if d == T_DIR:
+            there = [
+                (tr - 2 * KAPPA * pick(m["low"], zero, br), ti - 2 * KAPPA * pick(m["low"], zero, bi))
+                for (tr, ti), (br, bi) in zip(there, back[T_DIR])
+            ]
         pl.when(is_first[Y_DIR])(edges[d].wait_recv)
         scale = KAPPA * last_t if d == T_DIR else KAPPA
         extra = edge_term(d, edge_half[d]())
@@ -481,8 +517,10 @@
 
 
 def store_kernel(y_in, f_in, y_out, f_out, sems):
-    copies = [pltpu.make_async_copy(y_in, y_out, sems.at[4])]
-    copies += [pltpu.make_async_copy(f_in.at[d], f_out.at[d], sems.at[d]) for d in range(4)]
+    copies = [
+        pltpu.make_async_copy(f_in, f_out, sems.at[0]),
+        pltpu.make_async_copy(y_in, y_out, sems.at[1]),
+    ]
     for copy in copies:
         copy.start()
     for copy in copies:
@@ -504,12 +542,13 @@
             *faces,
             *faces,
             pltpu.VMEM((6, 8, 128), jnp.float32),
-            pltpu.VMEM((6, 8, 128), jnp.float32),
+            pltpu.VMEM((3, 8, 128), jnp.float32),
+            pltpu.VMEM((3, 8, 128), jnp.float32),
             pltpu.VMEM((6, 8, 128), jnp.float32),
             pltpu.SemaphoreType.DMA((5,)),
             pltpu.SemaphoreType.DMA((11,)),
             pltpu.SemaphoreType.DMA((11,)),
-            pltpu.SemaphoreType.REGULAR((2,)),
+            pltpu.SemaphoreType.REGULAR((4,)),
         ],
         compiler_params=pltpu.CompilerParams(collective_id=0, has_side_effects=True, vmem_limit_bytes=16 * 1024 * 1024),
         cost_estimate=pl.CostEstimate(flops=6_000_000, bytes_accessed=800_000, transcendentals=0),
@@ -522,7 +561,7 @@
         ),
         in_specs=[pl.BlockSpec(memory_space=pltpu.VMEM)] * 2,
         out_specs=(pl.BlockSpec(memory_space=pl.ANY),) * 2,
-        scratch_shapes=[pltpu.SemaphoreType.DMA((5,))],
+        scratch_shapes=[pltpu.SemaphoreType.DMA((2,))],
         compiler_params=pltpu.CompilerParams(vmem_limit_bytes=16 * 1024 * 1024),
         cost_estimate=pl.CostEstimate(flops=0, bytes_accessed=800_000, transcendentals=0),
     )(y, f)

time: 18.3 us -> 17.9 us (0.978)
  the two profiles are of different devices: /device:TPU:6 before, /device:TPU:25 now
where the time goes in v5:
time: 17.9 us; the launch traced here: 17.8 us
  Pallas kernels  17.1 us (96%)
  between operations  0.64 us (4%)
    pallas_call x1, Pallas kernels, body(): pl.pallas_call(kernel, out_shape=(pltpu.VMEM(x.shape, jnp.float32), pltpu...  16.4 us
    pallas_call x1, Pallas kernels, body(): pl.pallas_call(store_kernel, out_shape=(jax.ShapeDtypeStruct(x.shape, jnp...  0.76 us

profile of v5, /device:TPU:25, one launch (start us, length us, event | category | flops | bytes accessed | tf_op | source)
XLA Modules:
  0.0 17.8 jit_solution(7158195404994903253)
XLA Ops:
  0.6 16.4 %shard_map.41 = (f32[12,16,128]{2,1,0:T(8,128)S(1)}, f32[4,9,16,128]{3,2,1,0:T(8,128)S(1)}) custom-call(f32[12,16,128]{2,1,0:T(8,128)} %bitcast.5, f32[4,9,16,128]{3,2,1,0:T(8,128)} %bitcast.4), custom_call_target="tpu_custom_call" | custom-call | flops 6000000 | bytes 800000 | tf_op jit(solution)/shard_map/pallas_call | solution.py:534
  17.0 0.8 %shard_map.42 = (f32[12,16,128]{2,1,0:T(8,128)}, f32[4,9,16,128]{3,2,1,0:T(8,128)}) custom-call(f32[12,16,128]{2,1,0:T(8,128)S(1)} %get-tuple-element.6.y_in, f32[4,9,16,128]{3,2,1,0:T(8,128)S(1)} %get-tuple-element.7.f_in), custom_call_target="tpu_custom_call" | custom-call | bytes 800000 | tf_op jit(solution)/shard_map/pallas_call | solution.py:556

commit v6 on v5

--- a/solution.py
+++ b/solution.py
@@ -13,6 +13,9 @@
 AXES = {T_DIR: "ta", Z_DIR: "gz", Y_DIR: "gy"}
 FACES = (T_DIR, Z_DIR, Y_DIR)
 FACE_TILES = {T_DIR: 6, Z_DIR: 3, Y_DIR: 6}
+FACE_START = {T_DIR: 0, Z_DIR: 18, Y_DIR: 27}
+ALL_TILES = 45
+RECV_SEM = {(T_DIR, 0): 0, (T_DIR, 1): 0, (Z_DIR, 0): 1, (Z_DIR, 1): 1, (Y_DIR, 0): 2, (Y_DIR, 1): 3}
 
 
 def lane_roll(v, steps):
@@ -249,15 +252,21 @@
 def kernel(
     x_hbm, u_hbm, y_buf, f_buf,
     x_buf, u_buf,
-    st_t, st_z, st_y, rt_t, rt_z, rt_y, y_now, edge_out, edge_t, edge_z,
+    outbox, inbox, y_now, edge_out, edge_t, edge_z,
     load_sem, send_sem, recv_sem, here_sem,
 ):
-    send_buf = {T_DIR: st_t, Z_DIR: st_z, Y_DIR: st_y}
-    recv_buf = {T_DIR: rt_t, Z_DIR: rt_z, Y_DIR: rt_y}
-    x_load = pltpu.make_async_copy(x_hbm, x_buf, load_sem.at[4])
-    u_load = {d: pltpu.make_async_copy(u_hbm.at[d], u_buf.at[d], load_sem.at[d]) for d in range(4)}
-    x_load.start()
-    u_load[Y_DIR].start()
+    def face_of(box, d, slot, faces=1):
+        return box.at[pl.ds(FACE_START[d] + slot * FACE_TILES[d], faces * FACE_TILES[d])]
+
+    x_load = pltpu.make_async_copy(x_hbm, x_buf, load_sem.at[0])
+    y_load = pltpu.make_async_copy(u_hbm.at[Y_DIR], u_buf.at[Y_DIR], load_sem.at[1])
+    rest_load = pltpu.make_async_copy(u_hbm.at[pl.ds(0, 3)], u_buf.at[pl.ds(0, 3)], load_sem.at[2])
+    for s in range(4):
+        part = pl.ds(3 * s, 3)
+        pltpu.make_async_copy(x_hbm.at[part], x_buf.at[part], load_sem.at[0]).start()
+    for a in range(3):
+        part = (Y_DIR, pl.ds(3 * a, 3))
+        pltpu.make_async_copy(u_hbm.at[part], u_buf.at[part], load_sem.at[1]).start()
     me = {d: lax.axis_index(AXES[d]) for d in FACES}
     size = {d: lax.axis_size(AXES[d]) for d in FACES}
     ahead = {d: lax.rem(me[d] + 1, size[d]) for d in FACES}
@@ -284,15 +293,14 @@
 
     arrivals = 5 - sum(is_first[d].astype(jnp.int32) for d in FACES) + 3 * is_last_y.astype(jnp.int32)
     for d in (T_DIR, Z_DIR, X_DIR):
-        u_load[d].start()
-
-    def link(d, slot, there):
-        n = 3 * (d - 1) + slot
+        pltpu.make_async_copy(u_hbm.at[d], u_buf.at[d], load_sem.at[2]).start()
+
+    def link(d, slot, there, faces=1):
         return pltpu.make_async_remote_copy(
-            src_ref=send_buf[d].at[slot],
-            dst_ref=recv_buf[d].at[slot],
-            send_sem=send_sem.at[n],
-            recv_sem=recv_sem.at[n],
+            src_ref=face_of(outbox, d, slot, faces),
+            dst_ref=face_of(inbox, d, slot, faces),
+            send_sem=send_sem.at[0],
+            recv_sem=recv_sem.at[RECV_SEM.get((d, slot), 3 + d)],
             device_id={AXES[d]: there},
             device_id_type=MESH,
         )
@@ -300,20 +308,22 @@
     forward = {d: link(d, 0, behind[d]) for d in FACES}
     backward = {d: link(d, 1, ahead[d]) for d in FACES}
     upward = {d: link(d, 2, behind[d]) for d in FACES}
-
-    def edge_link(n, d, src, dst):
+    both = {d: link(d, 0, behind[d], 2) for d in (T_DIR, Z_DIR)}
+    all_sent = pltpu.make_async_copy(outbox, inbox, send_sem.at[0])
+
+    def edge_link(d, src, dst):
         return pltpu.make_async_remote_copy(
             src_ref=src,
             dst_ref=dst,
-            send_sem=send_sem.at[n],
-            recv_sem=recv_sem.at[n],
+            send_sem=send_sem.at[d - 1],
+            recv_sem=recv_sem.at[5 + d],
             device_id={AXES[d]: behind[d], AXES[Y_DIR]: ahead[Y_DIR]},
             device_id_type=MESH,
         )
 
     edges = {
-        T_DIR: edge_link(9, T_DIR, edge_out, edge_t),
-        Z_DIR: edge_link(10, Z_DIR, st_y.at[1, :, 0:2], edge_z.at[:, 6:8]),
+        T_DIR: edge_link(T_DIR, edge_out, edge_t),
+        Z_DIR: edge_link(Z_DIR, face_of(outbox, Y_DIR, 1).at[:, 0:2], edge_z.at[:, 6:8]),
     }
 
     here = {d: here_sem.at[d - 1] for d in FACES}
@@ -350,17 +360,18 @@
         return first.reshape(3, 3, 8, 128), second.reshape(3, 3, 8, 128)
 
     def prepare_backward(d):
-        u_load[d].wait()
         u[d] = links(d)
         plus[d] = project(d, 1, psi)
         back[d] = adjoint_times(u[d], plus[d])
-        stage_face(m, d, 1, back[d], send_buf[d].at[1])
-
+        stage_face(m, d, 1, back[d], face_of(outbox, d, 1))
+
+    y_load.wait()
     prepare_backward(Y_DIR)
 
     @pl.when(is_last_y)
     def _():
-        edge_out[...] = pick(m["low"], st_y[1, 0:3], lane_roll(st_y[1, 3:6], 64))
+        spins = both_spins(face_of(outbox, Y_DIR, 1))
+        edge_out[...] = pick(m["low"], spins[0], lane_roll(spins[1], 64))
         pl.semaphore_wait(barrier, arrivals)
         edges[Z_DIR].start()
         edges[T_DIR].start()
@@ -369,7 +380,8 @@
 
     for d in FACES:
         minus[d] = project(d, -1, psi)
-        stage_face(m, d, 0, minus[d], send_buf[d].at[0])
+        stage_face(m, d, 0, minus[d], face_of(outbox, d, 0))
+    rest_load.wait()
     for d in (T_DIR, Z_DIR):
         prepare_backward(d)
 
@@ -393,7 +405,6 @@
     zero = jnp.zeros((3, 8, 128), jnp.float32)
     hop = [(zero, zero)] * 4
     d = X_DIR
-    u_load[d].wait()
     u[d] = links(d)
     plus[d] = project(d, 1, psi)
     minus[d] = project(d, -1, psi)
@@ -403,40 +414,41 @@
     hop = add_spins(d, 1, hop, shift_x(m, adjoint_times(u[d], plus[d]), -1))
 
     def take_backward(d, hop):
-        backward[d].wait_recv()
-        there = shift_face(m, d, -1, back[d], recv_buf[d].at[1], behind_sign[d])
+        there = shift_face(m, d, -1, back[d], face_of(inbox, d, 1), behind_sign[d])
         return add_spins(d, 1, hop, there)
 
     def take_forward(d, hop):
-        forward[d].wait_recv()
-        there = shift_face(m, d, 1, minus[d], recv_buf[d].at[0], ahead_sign[d])
+        there = shift_face(m, d, 1, minus[d], face_of(inbox, d, 0), ahead_sign[d])
         moved[d] = link_times(u[d], there)
         return add_spins(d, -1, hop, moved[d])
 
     def wilson(hop):
         return [(pr - KAPPA * hr, pi - KAPPA * hi) for (pr, pi), (hr, hi) in zip(psi, hop)]
 
+    both[Z_DIR].wait_recv()
     hop = take_backward(Z_DIR, hop)
     hop = take_forward(Z_DIR, hop)
+    forward[Y_DIR].wait_recv()
     hop = take_forward(Y_DIR, hop)
     hop = add_spins(Y_DIR, 1, hop, local_y(m, back[Y_DIR]))
 
     @pl.when(jnp.logical_not(is_first[Y_DIR]))
     def _():
         backward[Y_DIR].wait_recv()
-        y_now[...] = rt_y[1]
+        y_now[...] = face_of(inbox, Y_DIR, 1)[...]
 
     hop = add_spins(Y_DIR, 1, hop, face_y(m["halo_now"], both_spins(y_now)))
 
     inner = [tuple(lane_roll(v, 64) for v in parts) for parts in minus[T_DIR]]
     inner = add_spins(T_DIR, -1, hop, link_times(u[T_DIR], inner))
-    stage_face(m, T_DIR, 0, project(T_DIR, 1, wilson(inner)), send_buf[T_DIR].at[2])
+    stage_face(m, T_DIR, 0, project(T_DIR, 1, wilson(inner)), face_of(outbox, T_DIR, 2))
     upward[T_DIR].start()
+    both[T_DIR].wait_recv()
     hop = take_backward(T_DIR, hop)
     hop = take_forward(T_DIR, hop)
     early = wilson(hop)
     for d in (Z_DIR, Y_DIR):
-        stage_face(m, d, 0, project(d, 1, early), send_buf[d].at[2])
+        stage_face(m, d, 0, project(d, 1, early), face_of(outbox, d, 2))
     upward[Z_DIR].start()
     pl.when(jnp.logical_not(is_first[Y_DIR]))(upward[Y_DIR].start)
 
@@ -446,7 +458,7 @@
         upward[Y_DIR].start()
         backward[Y_DIR].wait_recv()
 
-    late = face_y(m["halo_late"], both_spins(rt_y.at[1]))
+    late = face_y(m["halo_late"], both_spins(face_of(inbox, Y_DIR, 1)))
     missing = add_spins(Y_DIR, 1, [(zero, zero)] * 4, late)
     result = [
         (er - KAPPA * lr, ei - KAPPA * li) for (er, ei), (lr, li) in zip(early, missing)
@@ -480,7 +492,7 @@
     finish(d, outer(moved[d], project(d, -1, result)), shift_x(m, project(d, 1, result), 1))
     first = {d: outer(moved[d], project(d, -1, result)) for d in FACES}
     upward[Y_DIR].wait_recv()
-    there = shift_face(m, Y_DIR, 1, later[Y_DIR], recv_buf[Y_DIR].at[2], None)
+    there = shift_face(m, Y_DIR, 1, later[Y_DIR], face_of(inbox, Y_DIR, 2), None)
     there = [
         (tr - 2 * KAPPA * only(m["own_y"], br), ti - 2 * KAPPA * only(m["own_y"], bi))
         for (tr, ti), (br, bi) in zip(there, back[Y_DIR])
@@ -492,7 +504,7 @@
     }
     for d in (T_DIR, Z_DIR):
         upward[d].wait_recv()
-        there = shift_face(m, d, 1, later[d], recv_buf[d].at[2], ahead_sign[d])
+        there = shift_face(m, d, 1, later[d], face_of(inbox, d, 2), ahead_sign[d])
         if d == T_DIR:
             there = [
                 (tr - 2 * KAPPA * pick(m["low"], zero, br), ti - 2 * KAPPA * pick(m["low"], zero, bi))
@@ -505,10 +517,7 @@
             (tr - scale * er, ti - scale * ei) for (tr, ti), (er, ei) in zip(there, extra)
         ]
         finish(d, first[d], there)
-    for d in FACES:
-        forward[d].wait_send()
-        backward[d].wait_send()
-        upward[d].wait_send()
+    all_sent.wait()
 
     @pl.when(is_last_y)
     def _():
@@ -530,7 +539,6 @@
 def body(quark_field, gauge_links):
     x = quark_field.reshape(12, 16, 128)
     u = gauge_links.reshape(4, 9, 16, 128)
-    faces = [pltpu.VMEM((3, FACE_TILES[d], 8, 128), jnp.float32) for d in FACES]
     y, f = pl.pallas_call(
         kernel,
         out_shape=(pltpu.VMEM(x.shape, jnp.float32), pltpu.VMEM(u.shape, jnp.float32)),
@@ -539,15 +547,15 @@
         scratch_shapes=[
             pltpu.VMEM(x.shape, jnp.float32),
             pltpu.VMEM(u.shape, jnp.float32),
-            *faces,
-            *faces,
+            pltpu.VMEM((ALL_TILES, 8, 128), jnp.float32),
+            pltpu.VMEM((ALL_TILES, 8, 128), jnp.float32),
             pltpu.VMEM((6, 8, 128), jnp.float32),
             pltpu.VMEM((3, 8, 128), jnp.float32),
             pltpu.VMEM((3, 8, 128), jnp.float32),
             pltpu.VMEM((6, 8, 128), jnp.float32),
-            pltpu.SemaphoreType.DMA((5,)),
-            pltpu.SemaphoreType.DMA((11,)),
-            pltpu.SemaphoreType.DMA((11,)),
+            pltpu.SemaphoreType.DMA((3,)),
+            pltpu.SemaphoreType.DMA((3,)),
+            pltpu.SemaphoreType.DMA((9,)),
             pltpu.SemaphoreType.REGULAR((4,)),
         ],
         compiler_params=pltpu.CompilerParams(collective_id=0, has_side_effects=True, vmem_limit_bytes=16 * 1024 * 1024),

time: 17.9 us -> 17.8 us (level)
  the two profiles are of different devices: /device:TPU:25 before, /device:TPU:27 now
where the time goes in v6:
time: 17.8 us; the launch traced here: 17.7 us
  Pallas kernels  17 us (96%)
  between operations  0.64 us (4%)
    pallas_call x1, Pallas kernels, body(): pl.pallas_call(kernel, out_shape=(pltpu.VMEM(x.shape, jnp.float32), pltpu...  16.3 us
    pallas_call x1, Pallas kernels, body(): pl.pallas_call(store_kernel, out_shape=(jax.ShapeDtypeStruct(x.shape, jnp...  0.76 us

profile of v6, /device:TPU:27, one launch (start us, length us, event | category | flops | bytes accessed | tf_op | source)
XLA Modules:
  0.0 17.7 jit_solution(2397790031754754157)
XLA Ops:
  0.6 16.3 %shard_map.41 = (f32[12,16,128]{2,1,0:T(8,128)S(1)}, f32[4,9,16,128]{3,2,1,0:T(8,128)S(1)}) custom-call(f32[12,16,128]{2,1,0:T(8,128)} %bitcast.5, f32[4,9,16,128]{3,2,1,0:T(8,128)} %bitcast.4), custom_call_target="tpu_custom_call" | custom-call | flops 6000000 | bytes 800000 | tf_op jit(solution)/shard_map/pallas_call | solution.py:542
  16.9 0.8 %shard_map.42 = (f32[12,16,128]{2,1,0:T(8,128)}, f32[4,9,16,128]{3,2,1,0:T(8,128)}) custom-call(f32[12,16,128]{2,1,0:T(8,128)S(1)} %get-tuple-element.6.y_in, f32[4,9,16,128]{3,2,1,0:T(8,128)S(1)} %get-tuple-element.7.f_in), custom_call_target="tpu_custom_call" | custom-call | bytes 800000 | tf_op jit(solution)/shard_map/pallas_call | solution.py:564

commit v7 on v6

--- a/solution.py
+++ b/solution.py
@@ -16,6 +16,7 @@
 FACE_START = {T_DIR: 0, Z_DIR: 18, Y_DIR: 27}
 ALL_TILES = 45
 RECV_SEM = {(T_DIR, 0): 0, (T_DIR, 1): 0, (Z_DIR, 0): 1, (Z_DIR, 1): 1, (Y_DIR, 0): 2, (Y_DIR, 1): 3}
+RECV_UP, RECV_EDGE = 4, 5
 
 
 def lane_roll(v, steps):
@@ -258,15 +259,17 @@
     def face_of(box, d, slot, faces=1):
         return box.at[pl.ds(FACE_START[d] + slot * FACE_TILES[d], faces * FACE_TILES[d])]
 
-    x_load = pltpu.make_async_copy(x_hbm, x_buf, load_sem.at[0])
-    y_load = pltpu.make_async_copy(u_hbm.at[Y_DIR], u_buf.at[Y_DIR], load_sem.at[1])
-    rest_load = pltpu.make_async_copy(u_hbm.at[pl.ds(0, 3)], u_buf.at[pl.ds(0, 3)], load_sem.at[2])
+    first_load = pltpu.make_async_copy(u_hbm.at[pl.ds(0, 21)], u_buf.at[pl.ds(0, 21)], load_sem.at[0])
+    rest_load = pltpu.make_async_copy(u_hbm.at[pl.ds(0, 27)], u_buf.at[pl.ds(0, 27)], load_sem.at[1])
+
+    def load(source, target, start, count, sem):
+        part = pl.ds(start, count)
+        pltpu.make_async_copy(source.at[part], target.at[part], load_sem.at[sem]).start()
+
     for s in range(4):
-        part = pl.ds(3 * s, 3)
-        pltpu.make_async_copy(x_hbm.at[part], x_buf.at[part], load_sem.at[0]).start()
+        load(x_hbm, x_buf, 3 * s, 3, 0)
     for a in range(3):
-        part = (Y_DIR, pl.ds(3 * a, 3))
-        pltpu.make_async_copy(u_hbm.at[part], u_buf.at[part], load_sem.at[1]).start()
+        load(u_hbm, u_buf, 9 * Y_DIR + 3 * a, 3, 0)
     me = {d: lax.axis_index(AXES[d]) for d in FACES}
     size = {d: lax.axis_size(AXES[d]) for d in FACES}
     ahead = {d: lax.rem(me[d] + 1, size[d]) for d in FACES}
@@ -280,9 +283,12 @@
     def greet(where):
         pl.semaphore_signal(barrier, inc=1, device_id=where, device_id_type=MESH)
 
-    for d in (T_DIR, Z_DIR):
-        greet({AXES[d]: behind[d]})
-    for d in FACES:
+    odd = lax.rem(me[T_DIR], 2) == 1
+    plain = jnp.logical_not(is_last_y)
+    pl.when(plain | odd | is_first[T_DIR])(functools.partial(greet, {AXES[T_DIR]: behind[T_DIR]}))
+    pl.when(plain | is_first[Z_DIR])(functools.partial(greet, {AXES[Z_DIR]: behind[Z_DIR]}))
+    pl.when((plain | odd) & jnp.logical_not(is_last[T_DIR]))(functools.partial(greet, {AXES[T_DIR]: ahead[T_DIR]}))
+    for d in (Z_DIR, Y_DIR):
         pl.when(jnp.logical_not(is_last[d]))(functools.partial(greet, {AXES[d]: ahead[d]}))
 
     @pl.when(is_first[Y_DIR])
@@ -291,16 +297,24 @@
         for d in (T_DIR, Z_DIR):
             greet({AXES[d]: ahead[d], AXES[Y_DIR]: behind[Y_DIR]})
 
-    arrivals = 5 - sum(is_first[d].astype(jnp.int32) for d in FACES) + 3 * is_last_y.astype(jnp.int32)
+    def one(flag):
+        return flag.astype(jnp.int32)
+
+    plain_arrivals = 5 - sum(one(is_first[d]) for d in FACES)
+    late_t = jnp.where(odd, one(is_last[T_DIR]), 2 - one(is_first[T_DIR]))
+    late_arrivals = late_t + 1 + one(is_last[Z_DIR]) - one(is_first[Z_DIR]) + 4
+    late_replies = one(jnp.logical_not(is_last[Z_DIR])) + jnp.where(odd, 2 - one(is_last[T_DIR]), 0)
+    arrivals = jnp.where(is_last_y, late_arrivals, plain_arrivals)
+    replies = jnp.where(is_last_y, late_replies, 1)
     for d in (T_DIR, Z_DIR, X_DIR):
-        pltpu.make_async_copy(u_hbm.at[d], u_buf.at[d], load_sem.at[2]).start()
+        load(u_hbm, u_buf, 9 * d, 9, 1)
 
     def link(d, slot, there, faces=1):
         return pltpu.make_async_remote_copy(
             src_ref=face_of(outbox, d, slot, faces),
             dst_ref=face_of(inbox, d, slot, faces),
             send_sem=send_sem.at[0],
-            recv_sem=recv_sem.at[RECV_SEM.get((d, slot), 3 + d)],
+            recv_sem=recv_sem.at[RECV_SEM.get((d, slot), RECV_UP)],
             device_id={AXES[d]: there},
             device_id_type=MESH,
         )
@@ -309,14 +323,15 @@
     backward = {d: link(d, 1, ahead[d]) for d in FACES}
     upward = {d: link(d, 2, behind[d]) for d in FACES}
     both = {d: link(d, 0, behind[d], 2) for d in (T_DIR, Z_DIR)}
+    all_up = pltpu.make_async_copy(outbox.at[pl.ds(0, 15)], inbox.at[pl.ds(0, 15)], recv_sem.at[RECV_UP])
     all_sent = pltpu.make_async_copy(outbox, inbox, send_sem.at[0])
 
     def edge_link(d, src, dst):
         return pltpu.make_async_remote_copy(
             src_ref=src,
             dst_ref=dst,
-            send_sem=send_sem.at[d - 1],
-            recv_sem=recv_sem.at[5 + d],
+            send_sem=send_sem.at[1],
+            recv_sem=recv_sem.at[RECV_EDGE],
             device_id={AXES[d]: behind[d], AXES[Y_DIR]: ahead[Y_DIR]},
             device_id_type=MESH,
         )
@@ -325,9 +340,10 @@
         T_DIR: edge_link(T_DIR, edge_out, edge_t),
         Z_DIR: edge_link(Z_DIR, face_of(outbox, Y_DIR, 1).at[:, 0:2], edge_z.at[:, 6:8]),
     }
-
-    here = {d: here_sem.at[d - 1] for d in FACES}
-    here_ahead = here_sem.at[3]
+    both_edges = edge_link(T_DIR, y_now.at[:, 0:6], y_now.at[:, 0:6])
+
+    here = {T_DIR: here_sem.at[0], Z_DIR: here_sem.at[0], Y_DIR: here_sem.at[1]}
+    here_near = here_sem.at[2]
 
     def say_here():
         def say(sem, there):
@@ -336,11 +352,16 @@
         for d in FACES:
             pl.when(is_last[d])(functools.partial(say, here[d], {AXES[d]: ahead[d]}))
         there = {AXES[Y_DIR]: behind[Y_DIR]}
-        pl.when(jnp.logical_not(is_first[Y_DIR]))(functools.partial(say, here_ahead, there))
-
-    def greeted(d):
-        pl.semaphore_wait(here[d], 1)
-        forward[d].start()
+        pl.when(jnp.logical_not(is_first[Y_DIR]))(functools.partial(say, here_near, there))
+
+        @pl.when(is_last_y)
+        def _():
+            pl.when(jnp.logical_not(is_first[Z_DIR]))(functools.partial(say, here_near, {AXES[Z_DIR]: behind[Z_DIR]}))
+            even = jnp.logical_not(odd)
+            pl.when(even)(functools.partial(say, here_near, {AXES[T_DIR]: ahead[T_DIR]}))
+            pl.when(even & jnp.logical_not(is_first[T_DIR]))(
+                functools.partial(say, here_near, {AXES[T_DIR]: behind[T_DIR]})
+            )
 
     m = masks(is_first[Y_DIR].astype(jnp.int32), is_last_y.astype(jnp.int32))
     last_t = jnp.where(me[T_DIR] == size[T_DIR] - 1, -1.0, 1.0).astype(jnp.float32)
@@ -348,7 +369,7 @@
     ahead_sign = {T_DIR: last_t, Z_DIR: None, Y_DIR: None}
     behind_sign = {T_DIR: first_t, Z_DIR: None, Y_DIR: None}
 
-    x_load.wait()
+    first_load.wait()
     psi = [unpack(m, x_buf[3 * s:3 * s + 3, 0:8], x_buf[3 * s:3 * s + 3, 8:16]) for s in range(4)]
     minus = {}
     plus = {}
@@ -356,7 +377,7 @@
     back = {}
 
     def links(d):
-        first, second = unpack(m, u_buf[d, :, 0:8], u_buf[d, :, 8:16])
+        first, second = unpack(m, u_buf[9 * d:9 * d + 9, 0:8], u_buf[9 * d:9 * d + 9, 8:16])
         return first.reshape(3, 3, 8, 128), second.reshape(3, 3, 8, 128)
 
     def prepare_backward(d):
@@ -365,15 +386,14 @@
         back[d] = adjoint_times(u[d], plus[d])
         stage_face(m, d, 1, back[d], face_of(outbox, d, 1))
 
-    y_load.wait()
     prepare_backward(Y_DIR)
 
     @pl.when(is_last_y)
     def _():
+        pl.semaphore_wait(barrier, arrivals)
+        edges[Z_DIR].start()
         spins = both_spins(face_of(outbox, Y_DIR, 1))
         edge_out[...] = pick(m["low"], spins[0], lane_roll(spins[1], 64))
-        pl.semaphore_wait(barrier, arrivals)
-        edges[Z_DIR].start()
         edges[T_DIR].start()
         backward[Y_DIR].start()
         say_here()
@@ -390,16 +410,21 @@
         pl.semaphore_wait(barrier, arrivals)
         say_here()
 
+    pl.when(is_last_y & (replies > 0))(lambda: pl.semaphore_wait(here_near, replies))
     for d in (T_DIR, Z_DIR):
         backward[d].start()
     for d in FACES:
         pl.when(jnp.logical_not(is_first[d]))(forward[d].start)
-    for d in (T_DIR, Z_DIR):
-        pl.when(is_first[d])(functools.partial(greeted, d))
+
+    @pl.when(is_first[T_DIR] | is_first[Z_DIR])
+    def _():
+        pl.semaphore_wait(here[T_DIR], is_first[T_DIR].astype(jnp.int32) + is_first[Z_DIR].astype(jnp.int32))
+        for d in (T_DIR, Z_DIR):
+            pl.when(is_first[d])(forward[d].start)
 
     @pl.when(jnp.logical_not(is_last_y))
     def _():
-        pl.semaphore_wait(here_ahead, 1)
+        pl.semaphore_wait(here_near, replies)
         backward[Y_DIR].start()
 
     zero = jnp.zeros((3, 8, 128), jnp.float32)
@@ -454,7 +479,8 @@
 
     @pl.when(is_first[Y_DIR])
     def _():
-        greeted(Y_DIR)
+        pl.semaphore_wait(here[Y_DIR], 1)
+        forward[Y_DIR].start()
         upward[Y_DIR].start()
         backward[Y_DIR].wait_recv()
 
@@ -482,16 +508,16 @@
                     im = (0.5 * KAPPA) * (wi[a, b] + wi[b, a])
                 top = pack_first(m, re, im)
                 bottom = pack_second(m, re, im)
-                f_buf[d, 3 * a + b, 0:8] = top
-                f_buf[d, 3 * a + b, 8:16] = bottom
+                f_buf[9 * d + 3 * a + b, 0:8] = top
+                f_buf[9 * d + 3 * a + b, 8:16] = bottom
                 if a != b:
-                    f_buf[d, 3 * b + a, 0:8] = pick(m["low"], -top, top)
-                    f_buf[d, 3 * b + a, 8:16] = pick(m["low"], -bottom, bottom)
+                    f_buf[9 * d + 3 * b + a, 0:8] = pick(m["low"], -top, top)
+                    f_buf[9 * d + 3 * b + a, 8:16] = pick(m["low"], -bottom, bottom)
 
     d = X_DIR
     finish(d, outer(moved[d], project(d, -1, result)), shift_x(m, project(d, 1, result), 1))
     first = {d: outer(moved[d], project(d, -1, result)) for d in FACES}
-    upward[Y_DIR].wait_recv()
+    all_up.wait()
     there = shift_face(m, Y_DIR, 1, later[Y_DIR], face_of(inbox, Y_DIR, 2), None)
     there = [
         (tr - 2 * KAPPA * only(m["own_y"], br), ti - 2 * KAPPA * only(m["own_y"], bi))
@@ -502,15 +528,14 @@
         T_DIR: lambda: face_y(m["edge_t"], [lane_roll(edge_t[...], 64), edge_t[...]]),
         Z_DIR: lambda: face_y(m["edge_z"], both_spins(edge_z)),
     }
+    pl.when(is_first[Y_DIR])(both_edges.wait_recv)
     for d in (T_DIR, Z_DIR):
-        upward[d].wait_recv()
         there = shift_face(m, d, 1, later[d], face_of(inbox, d, 2), ahead_sign[d])
         if d == T_DIR:
             there = [
                 (tr - 2 * KAPPA * pick(m["low"], zero, br), ti - 2 * KAPPA * pick(m["low"], zero, bi))
                 for (tr, ti), (br, bi) in zip(there, back[T_DIR])
             ]
-        pl.when(is_first[Y_DIR])(edges[d].wait_recv)
         scale = KAPPA * last_t if d == T_DIR else KAPPA
         extra = edge_term(d, edge_half[d]())
         there = [
@@ -519,10 +544,7 @@
         finish(d, first[d], there)
     all_sent.wait()
 
-    @pl.when(is_last_y)
-    def _():
-        edges[T_DIR].wait_send()
-        edges[Z_DIR].wait_send()
+    pl.when(is_last_y)(both_edges.wait_send)
 
 
 def store_kernel(y_in, f_in, y_out, f_out, sems):
@@ -538,7 +560,7 @@
 
 def body(quark_field, gauge_links):
     x = quark_field.reshape(12, 16, 128)
-    u = gauge_links.reshape(4, 9, 16, 128)
+    u = gauge_links.reshape(36, 16, 128)
     y, f = pl.pallas_call(
         kernel,
         out_shape=(pltpu.VMEM(x.shape, jnp.float32), pltpu.VMEM(u.shape, jnp.float32)),
@@ -553,10 +575,10 @@
             pltpu.VMEM((3, 8, 128), jnp.float32),
             pltpu.VMEM((3, 8, 128), jnp.float32),
             pltpu.VMEM((6, 8, 128), jnp.float32),
-            pltpu.SemaphoreType.DMA((3,)),
-            pltpu.SemaphoreType.DMA((3,)),
-            pltpu.SemaphoreType.DMA((9,)),
-            pltpu.SemaphoreType.REGULAR((4,)),
+            pltpu.SemaphoreType.DMA((2,)),
+            pltpu.SemaphoreType.DMA((2,)),
+            pltpu.SemaphoreType.DMA((6,)),
+            pltpu.SemaphoreType.REGULAR((3,)),
         ],
         compiler_params=pltpu.CompilerParams(collective_id=0, has_side_effects=True, vmem_limit_bytes=16 * 1024 * 1024),
         cost_estimate=pl.CostEstimate(flops=6_000_000, bytes_accessed=800_000, transcendentals=0),

time: 17.8 us -> 17.7 us (level)
  the two profiles are of different devices: /device:TPU:27 before, /device:TPU:1 now
where the time goes in v7:
time: 17.7 us; the launch traced here: 17.5 us
  Pallas kernels  16.9 us (95%)
  between operations  0.64 us (4%)
    pallas_call x1, Pallas kernels, body(): pl.pallas_call(kernel, out_shape=(pltpu.VMEM(x.shape, jnp.float32), pltpu...  16.1 us
    pallas_call x1, Pallas kernels, body(): pl.pallas_call(store_kernel, out_shape=(jax.ShapeDtypeStruct(x.shape, jnp...  0.76 us

profile of v7, /device:TPU:1, one launch (start us, length us, event | category | flops | bytes accessed | tf_op | source)
XLA Modules:
  0.0 17.5 jit_solution(15313541196172373889)
XLA Ops:
  0.6 16.1 %shard_map.41 = (f32[12,16,128]{2,1,0:T(8,128)S(1)}, f32[36,16,128]{2,1,0:T(8,128)S(1)}) custom-call(f32[12,16,128]{2,1,0:T(8,128)} %bitcast.5, f32[36,16,128]{2,1,0:T(8,128)} %bitcast.4), custom_call_target="tpu_custom_call" | custom-call | flops 6000000 | bytes 800000 | tf_op jit(solution)/shard_map/pallas_call | solution.py:564
  16.7 0.8 %shard_map.42 = (f32[12,16,128]{2,1,0:T(8,128)}, f32[36,16,128]{2,1,0:T(8,128)}) custom-call(f32[12,16,128]{2,1,0:T(8,128)S(1)} %get-tuple-element.6.y_in, f32[36,16,128]{2,1,0:T(8,128)S(1)} %get-tuple-element.7.f_in), custom_call_target="tpu_custom_call" | custom-call | bytes 800000 | tf_op jit(solution)/shard_map/pallas_call | solution.py:586

commit v8 on v7

--- a/solution.py
+++ b/solution.py
@@ -16,7 +16,7 @@
 FACE_START = {T_DIR: 0, Z_DIR: 18, Y_DIR: 27}
 ALL_TILES = 45
 RECV_SEM = {(T_DIR, 0): 0, (T_DIR, 1): 0, (Z_DIR, 0): 1, (Z_DIR, 1): 1, (Y_DIR, 0): 2, (Y_DIR, 1): 3}
-RECV_UP, RECV_EDGE = 4, 5
+RECV_UP, RECV_EDGE = 4, {T_DIR: 5, Z_DIR: 6}
 
 
 def lane_roll(v, steps):
@@ -266,8 +266,8 @@
         part = pl.ds(start, count)
         pltpu.make_async_copy(source.at[part], target.at[part], load_sem.at[sem]).start()
 
-    for s in range(4):
-        load(x_hbm, x_buf, 3 * s, 3, 0)
+    for s in range(3):
+        load(x_hbm, x_buf, 4 * s, 4, 0)
     for a in range(3):
         load(u_hbm, u_buf, 9 * Y_DIR + 3 * a, 3, 0)
     me = {d: lax.axis_index(AXES[d]) for d in FACES}
@@ -284,10 +284,11 @@
         pl.semaphore_signal(barrier, inc=1, device_id=where, device_id_type=MESH)
 
     odd = lax.rem(me[T_DIR], 2) == 1
+    greeter = odd ^ (me[Z_DIR] < size[Z_DIR] // 2)
     plain = jnp.logical_not(is_last_y)
-    pl.when(plain | odd | is_first[T_DIR])(functools.partial(greet, {AXES[T_DIR]: behind[T_DIR]}))
+    pl.when(plain | greeter | is_first[T_DIR])(functools.partial(greet, {AXES[T_DIR]: behind[T_DIR]}))
     pl.when(plain | is_first[Z_DIR])(functools.partial(greet, {AXES[Z_DIR]: behind[Z_DIR]}))
-    pl.when((plain | odd) & jnp.logical_not(is_last[T_DIR]))(functools.partial(greet, {AXES[T_DIR]: ahead[T_DIR]}))
+    pl.when((plain | greeter) & jnp.logical_not(is_last[T_DIR]))(functools.partial(greet, {AXES[T_DIR]: ahead[T_DIR]}))
     for d in (Z_DIR, Y_DIR):
         pl.when(jnp.logical_not(is_last[d]))(functools.partial(greet, {AXES[d]: ahead[d]}))
 
@@ -301,9 +302,9 @@
         return flag.astype(jnp.int32)
 
     plain_arrivals = 5 - sum(one(is_first[d]) for d in FACES)
-    late_t = jnp.where(odd, one(is_last[T_DIR]), 2 - one(is_first[T_DIR]))
+    late_t = jnp.where(greeter, one(odd & is_last[T_DIR]), 2 - one(is_first[T_DIR]))
     late_arrivals = late_t + 1 + one(is_last[Z_DIR]) - one(is_first[Z_DIR]) + 4
-    late_replies = one(jnp.logical_not(is_last[Z_DIR])) + jnp.where(odd, 2 - one(is_last[T_DIR]), 0)
+    late_replies = one(jnp.logical_not(is_last[Z_DIR])) + jnp.where(greeter, 2 - one(is_last[T_DIR]) - one(is_first[T_DIR]), 0)
     arrivals = jnp.where(is_last_y, late_arrivals, plain_arrivals)
     replies = jnp.where(is_last_y, late_replies, 1)
     for d in (T_DIR, Z_DIR, X_DIR):
@@ -331,7 +332,7 @@
             src_ref=src,
             dst_ref=dst,
             send_sem=send_sem.at[1],
-            recv_sem=recv_sem.at[RECV_EDGE],
+            recv_sem=recv_sem.at[RECV_EDGE[d]],
             device_id={AXES[d]: behind[d], AXES[Y_DIR]: ahead[Y_DIR]},
             device_id_type=MESH,
         )
@@ -357,9 +358,11 @@
         @pl.when(is_last_y)
         def _():
             pl.when(jnp.logical_not(is_first[Z_DIR]))(functools.partial(say, here_near, {AXES[Z_DIR]: behind[Z_DIR]}))
-            even = jnp.logical_not(odd)
-            pl.when(even)(functools.partial(say, here_near, {AXES[T_DIR]: ahead[T_DIR]}))
-            pl.when(even & jnp.logical_not(is_first[T_DIR]))(
+            greeted = jnp.logical_not(greeter)
+            pl.when(greeted & jnp.logical_not(is_last[T_DIR]))(
+                functools.partial(say, here_near, {AXES[T_DIR]: ahead[T_DIR]})
+            )
+            pl.when(greeted & jnp.logical_not(is_first[T_DIR]))(
                 functools.partial(say, here_near, {AXES[T_DIR]: behind[T_DIR]})
             )
 
@@ -528,7 +531,6 @@
         T_DIR: lambda: face_y(m["edge_t"], [lane_roll(edge_t[...], 64), edge_t[...]]),
         Z_DIR: lambda: face_y(m["edge_z"], both_spins(edge_z)),
     }
-    pl.when(is_first[Y_DIR])(both_edges.wait_recv)
     for d in (T_DIR, Z_DIR):
         there = shift_face(m, d, 1, later[d], face_of(inbox, d, 2), ahead_sign[d])
         if d == T_DIR:
@@ -536,6 +538,7 @@
                 (tr - 2 * KAPPA * pick(m["low"], zero, br), ti - 2 * KAPPA * pick(m["low"], zero, bi))
                 for (tr, ti), (br, bi) in zip(there, back[T_DIR])
             ]
+        pl.when(is_first[Y_DIR])(edges[d].wait_recv)
         scale = KAPPA * last_t if d == T_DIR else KAPPA
         extra = edge_term(d, edge_half[d]())
         there = [
@@ -577,7 +580,7 @@
             pltpu.VMEM((6, 8, 128), jnp.float32),
             pltpu.SemaphoreType.DMA((2,)),
             pltpu.SemaphoreType.DMA((2,)),
-            pltpu.SemaphoreType.DMA((6,)),
+            pltpu.SemaphoreType.DMA((7,)),
             pltpu.SemaphoreType.REGULAR((3,)),
         ],
         compiler_params=pltpu.CompilerParams(collective_id=0, has_side_effects=True, vmem_limit_bytes=16 * 1024 * 1024),

time: 17.7 us -> 17.4 us (0.983)
  the two profiles are of different devices: /device:TPU:1 before, /device:TPU:23 now
where the time goes in v8:
time: 17.4 us; the launch traced here: 17.2 us
  Pallas kernels  16.6 us (95%)
  between operations  0.64 us (4%)
    pallas_call x1, Pallas kernels, body(): pl.pallas_call(kernel, out_shape=(pltpu.VMEM(x.shape, jnp.float32), pltpu...  15.8 us
    pallas_call x1, Pallas kernels, body(): pl.pallas_call(store_kernel, out_shape=(jax.ShapeDtypeStruct(x.shape, jnp...  0.76 us

profile of v8, /device:TPU:23, one launch (start us, length us, event | category | flops | bytes accessed | tf_op | source)
XLA Modules:
  0.0 17.2 jit_solution(7613279014407617751)
XLA Ops:
  0.6 15.8 %shard_map.41 = (f32[12,16,128]{2,1,0:T(8,128)S(1)}, f32[36,16,128]{2,1,0:T(8,128)S(1)}) custom-call(f32[12,16,128]{2,1,0:T(8,128)} %bitcast.5, f32[36,16,128]{2,1,0:T(8,128)} %bitcast.4), custom_call_target="tpu_custom_call" | custom-call | flops 6000000 | bytes 800000 | tf_op jit(solution)/shard_map/pallas_call | solution.py:567
  16.4 0.8 %shard_map.42 = (f32[12,16,128]{2,1,0:T(8,128)}, f32[36,16,128]{2,1,0:T(8,128)}) custom-call(f32[12,16,128]{2,1,0:T(8,128)S(1)} %get-tuple-element.6.y_in, f32[36,16,128]{2,1,0:T(8,128)S(1)} %get-tuple-element.7.f_in), custom_call_target="tpu_custom_call" | custom-call | bytes 800000 | tf_op jit(solution)/shard_map/pallas_call | solution.py:589

commit v9 on v8

--- a/solution.py
+++ b/solution.py
@@ -250,8 +250,30 @@
     return project(direction, 1, [h0, h1, h1, (-h0[0], -h0[1])])
 
 
+def write_force(low, u, plus, first, later_there, f_buf, start):
+    second = outer(link_times(u, later_there), plus)
+    wr, wi = c_add(first, second)
+    third = (wi[0, 0] + wi[1, 1] + wi[2, 2]) / 3.0
+    m = {"low": low}
+    for a in range(3):
+        for b in range(a, 3):
+            if a == b:
+                im = KAPPA * (wi[a, a] - third)
+                re = jnp.zeros_like(im)
+            else:
+                re = (0.5 * KAPPA) * (wr[a, b] - wr[b, a])
+                im = (0.5 * KAPPA) * (wi[a, b] + wi[b, a])
+            top = pack_first(m, re, im)
+            bottom = pack_second(m, re, im)
+            f_buf[start + 3 * a + b, 0:8] = top
+            f_buf[start + 3 * a + b, 8:16] = bottom
+            if a != b:
+                f_buf[start + 3 * b + a, 0:8] = pick(low, -top, top)
+                f_buf[start + 3 * b + a, 8:16] = pick(low, -bottom, bottom)
+
+
 def kernel(
-    x_hbm, u_hbm, y_buf, f_buf,
+    x_hbm, u_hbm, y_buf, f_buf, z_buf,
     x_buf, u_buf,
     outbox, inbox, y_now, edge_out, edge_t, edge_z,
     load_sem, send_sem, recv_sem, here_sem,
@@ -498,24 +520,7 @@
         y_buf[3 * s:3 * s + 3, 8:16] = pack_second(m, re, im)
 
     def finish(d, first, later_there):
-        second = outer(link_times(u[d], later_there), plus[d])
-        wr, wi = c_add(first, second)
-        third = (wi[0, 0] + wi[1, 1] + wi[2, 2]) / 3.0
-        for a in range(3):
-            for b in range(a, 3):
-                if a == b:
-                    im = KAPPA * (wi[a, a] - third)
-                    re = jnp.zeros_like(im)
-                else:
-                    re = (0.5 * KAPPA) * (wr[a, b] - wr[b, a])
-                    im = (0.5 * KAPPA) * (wi[a, b] + wi[b, a])
-                top = pack_first(m, re, im)
-                bottom = pack_second(m, re, im)
-                f_buf[9 * d + 3 * a + b, 0:8] = top
-                f_buf[9 * d + 3 * a + b, 8:16] = bottom
-                if a != b:
-                    f_buf[9 * d + 3 * b + a, 0:8] = pick(m["low"], -top, top)
-                    f_buf[9 * d + 3 * b + a, 8:16] = pick(m["low"], -bottom, bottom)
+        write_force(m["low"], u[d], plus[d], first, later_there, f_buf, 9 * d)
 
     d = X_DIR
     finish(d, outer(moved[d], project(d, -1, result)), shift_x(m, project(d, 1, result), 1))
@@ -527,6 +532,9 @@
         for (tr, ti), (br, bi) in zip(there, back[Y_DIR])
     ]
     finish(Y_DIR, first[Y_DIR], there)
+    z_buf[12:30] = jnp.concatenate([part.reshape(9, 8, 128) for part in u[Z_DIR]])
+    z_buf[30:48] = jnp.concatenate([part.reshape(9, 8, 128) for part in first[Z_DIR]])
+    z_buf[48:60] = jnp.concatenate([part for half in plus[Z_DIR] for part in half])
     edge_half = {
         T_DIR: lambda: face_y(m["edge_t"], [lane_roll(edge_t[...], 64), edge_t[...]]),
         Z_DIR: lambda: face_y(m["edge_z"], both_spins(edge_z)),
@@ -544,31 +552,46 @@
         there = [
             (tr - scale * er, ti - scale * ei) for (tr, ti), (er, ei) in zip(there, extra)
         ]
-        finish(d, first[d], there)
+        if d == T_DIR:
+            finish(d, first[d], there)
+        else:
+            for n, part in enumerate([part for half in there for part in half]):
+                z_buf[3 * n:3 * n + 3] = part
     all_sent.wait()
 
     pl.when(is_last_y)(both_edges.wait_send)
 
 
-def store_kernel(y_in, f_in, y_out, f_out, sems):
-    copies = [
-        pltpu.make_async_copy(f_in, f_out, sems.at[0]),
-        pltpu.make_async_copy(y_in, y_out, sems.at[1]),
-    ]
-    for copy in copies:
-        copy.start()
-    for copy in copies:
-        copy.wait()
+def store_kernel(y_in, f_in, z_in, y_out, f_out, fz_buf, sems):
+    def store(source, start, count):
+        pltpu.make_async_copy(source, f_out.at[pl.ds(start, count)], sems.at[0]).start()
+
+    store(f_in.at[pl.ds(0, 18)], 0, 18)
+    store(f_in.at[pl.ds(27, 9)], 27, 9)
+    y_store = pltpu.make_async_copy(y_in, y_out, sems.at[1])
+    y_store.start()
+
+    def halves(start):
+        return [tuple(z_in[start + 6 * s + 3 * p:start + 6 * s + 3 * p + 3] for p in range(2)) for s in range(2)]
+
+    def matrix(start):
+        return tuple(z_in[start + 9 * p:start + 9 * p + 9].reshape(3, 3, 8, 128) for p in range(2))
+
+    low = lax.broadcasted_iota(jnp.int32, (8, 128), 1) < 64
+    write_force(low, matrix(12), halves(48), matrix(30), halves(0), fz_buf, 0)
+    store(fz_buf, 18, 9)
+    pltpu.make_async_copy(f_in, f_out, sems.at[0]).wait()
+    y_store.wait()
 
 
 def body(quark_field, gauge_links):
     x = quark_field.reshape(12, 16, 128)
     u = gauge_links.reshape(36, 16, 128)
-    y, f = pl.pallas_call(
+    y, f, z = pl.pallas_call(
         kernel,
-        out_shape=(pltpu.VMEM(x.shape, jnp.float32), pltpu.VMEM(u.shape, jnp.float32)),
+        out_shape=tuple(pltpu.VMEM(shape, jnp.float32) for shape in (x.shape, u.shape, (60, 8, 128))),
         in_specs=[pl.BlockSpec(memory_space=pltpu.HBM)] * 2,
-        out_specs=(pl.BlockSpec(memory_space=pltpu.VMEM),) * 2,
+        out_specs=(pl.BlockSpec(memory_space=pltpu.VMEM),) * 3,
         scratch_shapes=[
             pltpu.VMEM(x.shape, jnp.float32),
             pltpu.VMEM(u.shape, jnp.float32),
@@ -592,12 +615,12 @@
             jax.ShapeDtypeStruct(x.shape, jnp.float32),
             jax.ShapeDtypeStruct(u.shape, jnp.float32),
         ),
-        in_specs=[pl.BlockSpec(memory_space=pltpu.VMEM)] * 2,
+        in_specs=[pl.BlockSpec(memory_space=pltpu.VMEM)] * 3,
         out_specs=(pl.BlockSpec(memory_space=pl.ANY),) * 2,
-        scratch_shapes=[pltpu.SemaphoreType.DMA((2,))],
+        scratch_shapes=[pltpu.VMEM((9, 16, 128), jnp.float32), pltpu.SemaphoreType.DMA((2,))],
         compiler_params=pltpu.CompilerParams(vmem_limit_bytes=16 * 1024 * 1024),
-        cost_estimate=pl.CostEstimate(flops=0, bytes_accessed=800_000, transcendentals=0),
-    )(y, f)
+        cost_estimate=pl.CostEstimate(flops=400_000, bytes_accessed=800_000, transcendentals=0),
+    )(y, f, z)
     return y.reshape(quark_field.shape), f.reshape(gauge_links.shape)
 
 

time: 17.4 us -> 17.3 us (level)
  no operation moved by 1% of the time
where the time goes in v9:
time: 17.3 us; the launch traced here: 17.1 us
  Pallas kernels  16.5 us (95%)
  between operations  0.64 us (4%)
    pallas_call x1, Pallas kernels, body(): pl.pallas_call(kernel, out_shape=tuple((pltpu.VMEM(shape, jnp.float32) fo...  15.7 us
    pallas_call x1, Pallas kernels, body(): pl.pallas_call(store_kernel, out_shape=(jax.ShapeDtypeStruct(x.shape, jnp...  0.77 us

profile of v9, /device:TPU:23, one launch (start us, length us, event | category | flops | bytes accessed | tf_op | source)
XLA Modules:
  0.0 17.1 jit_solution(6840830205864330177)
XLA Ops:
  0.6 15.7 %shard_map.41 = (f32[12,16,128]{2,1,0:T(8,128)S(1)}, f32[36,16,128]{2,1,0:T(8,128)S(1)}, f32[60,8,128]{2,1,0:T(8,128)S(1)}) custom-call(f32[12,16,128]{2,1,0:T(8,128)} %bitcast.5, f32[36,16,128]{2,1,0:T(8,128)} %bitcast.4), custom_call_target="tpu_custom_call" | custom-call | flops 6000000 | bytes 800000 | tf_op jit(solution)/shard_map/pallas_call | solution.py:590
  16.3 0.8 %shard_map.42 = (f32[12,16,128]{2,1,0:T(8,128)}, f32[36,16,128]{2,1,0:T(8,128)}) custom-call(f32[12,16,128]{2,1,0:T(8,128)S(1)} %get-tuple-element.7.y_in, f32[36,16,128]{2,1,0:T(8,128)S(1)} %get-tuple-element.8.f_in, f32[60,8,128]{2,1,0:T(8,128)S(1)} %get-tuple-element.9.z_in), custom_call_target="tpu_custom_call" | custom-call | flops 400000 | bytes 800000 | tf_op jit(solution)/shard_map/pallas_call | solution.py:612

commit v10 on v9

--- a/solution.py
+++ b/solution.py
@@ -15,8 +15,8 @@
 FACE_TILES = {T_DIR: 6, Z_DIR: 3, Y_DIR: 6}
 FACE_START = {T_DIR: 0, Z_DIR: 18, Y_DIR: 27}
 ALL_TILES = 45
-RECV_SEM = {(T_DIR, 0): 0, (T_DIR, 1): 0, (Z_DIR, 0): 1, (Z_DIR, 1): 1, (Y_DIR, 0): 2, (Y_DIR, 1): 3}
-RECV_UP, RECV_EDGE = 4, {T_DIR: 5, Z_DIR: 6}
+RECV_SEM = {(T_DIR, 0): 0, (T_DIR, 1): 0, (Z_DIR, 0): 1, (Z_DIR, 1): 1, (Y_DIR, 0): 1, (Y_DIR, 1): 2}
+RECV_UP, RECV_EDGE = 3, {T_DIR: 4, Z_DIR: 5}
 
 
 def lane_roll(v, steps):
@@ -273,11 +273,13 @@
 
 
 def kernel(
-    x_hbm, u_hbm, y_buf, f_buf, z_buf,
+    x_hbm, u_hbm, out_buf, z_buf,
     x_buf, u_buf,
     outbox, inbox, y_now, edge_out, edge_t, edge_z,
     load_sem, send_sem, recv_sem, here_sem,
 ):
+    y_buf, f_buf = out_buf.at[pl.ds(0, 12)], out_buf.at[pl.ds(12, 36)]
+
     def face_of(box, d, slot, faces=1):
         return box.at[pl.ds(FACE_START[d] + slot * FACE_TILES[d], faces * FACE_TILES[d])]
 
@@ -345,7 +347,8 @@
     forward = {d: link(d, 0, behind[d]) for d in FACES}
     backward = {d: link(d, 1, ahead[d]) for d in FACES}
     upward = {d: link(d, 2, behind[d]) for d in FACES}
-    both = {d: link(d, 0, behind[d], 2) for d in (T_DIR, Z_DIR)}
+    both_t = link(T_DIR, 0, behind[T_DIR], 2)
+    z_and_y = pltpu.make_async_copy(outbox.at[pl.ds(0, 12)], inbox.at[pl.ds(0, 12)], recv_sem.at[RECV_SEM[Z_DIR, 0]])
     all_up = pltpu.make_async_copy(outbox.at[pl.ds(0, 15)], inbox.at[pl.ds(0, 15)], recv_sem.at[RECV_UP])
     all_sent = pltpu.make_async_copy(outbox, inbox, send_sem.at[0])
 
@@ -475,10 +478,9 @@
     def wilson(hop):
         return [(pr - KAPPA * hr, pi - KAPPA * hi) for (pr, pi), (hr, hi) in zip(psi, hop)]
 
-    both[Z_DIR].wait_recv()
+    z_and_y.wait()
     hop = take_backward(Z_DIR, hop)
     hop = take_forward(Z_DIR, hop)
-    forward[Y_DIR].wait_recv()
     hop = take_forward(Y_DIR, hop)
     hop = add_spins(Y_DIR, 1, hop, local_y(m, back[Y_DIR]))
 
@@ -493,7 +495,7 @@
     inner = add_spins(T_DIR, -1, hop, link_times(u[T_DIR], inner))
     stage_face(m, T_DIR, 0, project(T_DIR, 1, wilson(inner)), face_of(outbox, T_DIR, 2))
     upward[T_DIR].start()
-    both[T_DIR].wait_recv()
+    both_t.wait_recv()
     hop = take_backward(T_DIR, hop)
     hop = take_forward(T_DIR, hop)
     early = wilson(hop)
@@ -562,14 +564,13 @@
     pl.when(is_last_y)(both_edges.wait_send)
 
 
-def store_kernel(y_in, f_in, z_in, y_out, f_out, fz_buf, sems):
-    def store(source, start, count):
-        pltpu.make_async_copy(source, f_out.at[pl.ds(start, count)], sems.at[0]).start()
-
-    store(f_in.at[pl.ds(0, 18)], 0, 18)
-    store(f_in.at[pl.ds(27, 9)], 27, 9)
-    y_store = pltpu.make_async_copy(y_in, y_out, sems.at[1])
-    y_store.start()
+def store_kernel(out_in, z_in, y_out, f_out, fz_buf, sem):
+    def store(source, target):
+        pltpu.make_async_copy(source, target, sem).start()
+
+    store(out_in.at[pl.ds(12, 18)], f_out.at[pl.ds(0, 18)])
+    store(out_in.at[pl.ds(39, 9)], f_out.at[pl.ds(27, 9)])
+    store(out_in.at[pl.ds(0, 12)], y_out)
 
     def halves(start):
         return [tuple(z_in[start + 6 * s + 3 * p:start + 6 * s + 3 * p + 3] for p in range(2)) for s in range(2)]
@@ -579,19 +580,18 @@
 
     low = lax.broadcasted_iota(jnp.int32, (8, 128), 1) < 64
     write_force(low, matrix(12), halves(48), matrix(30), halves(0), fz_buf, 0)
-    store(fz_buf, 18, 9)
-    pltpu.make_async_copy(f_in, f_out, sems.at[0]).wait()
-    y_store.wait()
+    store(fz_buf, f_out.at[pl.ds(18, 9)])
+    pltpu.make_async_copy(out_in, out_in, sem).wait()
 
 
 def body(quark_field, gauge_links):
     x = quark_field.reshape(12, 16, 128)
     u = gauge_links.reshape(36, 16, 128)
-    y, f, z = pl.pallas_call(
+    out, z = pl.pallas_call(
         kernel,
-        out_shape=tuple(pltpu.VMEM(shape, jnp.float32) for shape in (x.shape, u.shape, (60, 8, 128))),
+        out_shape=tuple(pltpu.VMEM(shape, jnp.float32) for shape in ((48, 16, 128), (60, 8, 128))),
         in_specs=[pl.BlockSpec(memory_space=pltpu.HBM)] * 2,
-        out_specs=(pl.BlockSpec(memory_space=pltpu.VMEM),) * 3,
+        out_specs=(pl.BlockSpec(memory_space=pltpu.VMEM),) * 2,
         scratch_shapes=[
             pltpu.VMEM(x.shape, jnp.float32),
             pltpu.VMEM(u.shape, jnp.float32),
@@ -603,7 +603,7 @@
             pltpu.VMEM((6, 8, 128), jnp.float32),
             pltpu.SemaphoreType.DMA((2,)),
             pltpu.SemaphoreType.DMA((2,)),
-            pltpu.SemaphoreType.DMA((7,)),
+            pltpu.SemaphoreType.DMA((6,)),
             pltpu.SemaphoreType.REGULAR((3,)),
         ],
         compiler_params=pltpu.CompilerParams(collective_id=0, has_side_effects=True, vmem_limit_bytes=16 * 1024 * 1024),
@@ -615,12 +615,12 @@
             jax.ShapeDtypeStruct(x.shape, jnp.float32),
             jax.ShapeDtypeStruct(u.shape, jnp.float32),
         ),
-        in_specs=[pl.BlockSpec(memory_space=pltpu.VMEM)] * 3,
+        in_specs=[pl.BlockSpec(memory_space=pltpu.VMEM)] * 2,
         out_specs=(pl.BlockSpec(memory_space=pl.ANY),) * 2,
-        scratch_shapes=[pltpu.VMEM((9, 16, 128), jnp.float32), pltpu.SemaphoreType.DMA((2,))],
+        scratch_shapes=[pltpu.VMEM((9, 16, 128), jnp.float32), pltpu.SemaphoreType.DMA],
         compiler_params=pltpu.CompilerParams(vmem_limit_bytes=16 * 1024 * 1024),
         cost_estimate=pl.CostEstimate(flops=400_000, bytes_accessed=800_000, transcendentals=0),
-    )(y, f, z)
+    )(out, z)
     return y.reshape(quark_field.shape), f.reshape(gauge_links.shape)
 
 

time: 17.3 us -> 17.3 us (level)
  no operation moved by 1% of the time
where the time goes in v10:
time: 17.3 us; the launch traced here: 17.1 us
  Pallas kernels  16.4 us (95%)
  between operations  0.64 us (4%)
    pallas_call x1, Pallas kernels, body(): pl.pallas_call(kernel, out_shape=tuple((pltpu.VMEM(shape, jnp.float32) fo...  15.7 us
    pallas_call x1, Pallas kernels, body(): pl.pallas_call(store_kernel, out_shape=(jax.ShapeDtypeStruct(x.shape, jnp...  0.76 us

profile of v10, /device:TPU:23, one launch (start us, length us, event | category | flops | bytes accessed | tf_op | source)
XLA Modules:
  0.0 17.1 jit_solution(20518416186482626)
XLA Ops:
  0.6 15.7 %shard_map.41 = (f32[48,16,128]{2,1,0:T(8,128)S(1)}, f32[60,8,128]{2,1,0:T(8,128)S(1)}) custom-call(f32[12,16,128]{2,1,0:T(8,128)} %bitcast.5, f32[36,16,128]{2,1,0:T(8,128)} %bitcast.4), custom_call_target="tpu_custom_call" | custom-call | flops 6000000 | bytes 800000 | tf_op jit(solution)/shard_map/pallas_call | solution.py:590
  16.3 0.8 %shard_map.42 = (f32[12,16,128]{2,1,0:T(8,128)}, f32[36,16,128]{2,1,0:T(8,128)}) custom-call(f32[48,16,128]{2,1,0:T(8,128)S(1)} %get-tuple-element.6.out_in, f32[60,8,128]{2,1,0:T(8,128)S(1)} %get-tuple-element.7.z_in), custom_call_target="tpu_custom_call" | custom-call | flops 400000 | bytes 800000 | tf_op jit(solution)/shard_map/pallas_call | solution.py:612

commit v11 on v10

--- a/solution.py
+++ b/solution.py
@@ -548,17 +548,20 @@
                 (tr - 2 * KAPPA * pick(m["low"], zero, br), ti - 2 * KAPPA * pick(m["low"], zero, bi))
                 for (tr, ti), (br, bi) in zip(there, back[T_DIR])
             ]
+        if d == Z_DIR:
+            for n, part in enumerate([part for half in there for part in half]):
+                z_buf[3 * n:3 * n + 3] = part
         pl.when(is_first[Y_DIR])(edges[d].wait_recv)
-        scale = KAPPA * last_t if d == T_DIR else KAPPA
+        if d == Z_DIR:
+            for n, part in enumerate([part for half in edge_half[d]() for part in half]):
+                z_buf[60 + 3 * n:63 + 3 * n] = part
+            break
+        scale = KAPPA * last_t
         extra = edge_term(d, edge_half[d]())
         there = [
             (tr - scale * er, ti - scale * ei) for (tr, ti), (er, ei) in zip(there, extra)
         ]
-        if d == T_DIR:
-            finish(d, first[d], there)
-        else:
-            for n, part in enumerate([part for half in there for part in half]):
-                z_buf[3 * n:3 * n + 3] = part
+        finish(d, first[d], there)
     all_sent.wait()
 
     pl.when(is_last_y)(both_edges.wait_send)
@@ -579,7 +582,10 @@
         return tuple(z_in[start + 9 * p:start + 9 * p + 9].reshape(3, 3, 8, 128) for p in range(2))
 
     low = lax.broadcasted_iota(jnp.int32, (8, 128), 1) < 64
-    write_force(low, matrix(12), halves(48), matrix(30), halves(0), fz_buf, 0)
+    there = [
+        (tr - KAPPA * er, ti - KAPPA * ei) for (tr, ti), (er, ei) in zip(halves(0), edge_term(Z_DIR, halves(60)))
+    ]
+    write_force(low, matrix(12), halves(48), matrix(30), there, fz_buf, 0)
     store(fz_buf, f_out.at[pl.ds(18, 9)])
     pltpu.make_async_copy(out_in, out_in, sem).wait()
 
@@ -589,7 +595,7 @@
     u = gauge_links.reshape(36, 16, 128)
     out, z = pl.pallas_call(
         kernel,
-        out_shape=tuple(pltpu.VMEM(shape, jnp.float32) for shape in ((48, 16, 128), (60, 8, 128))),
+        out_shape=tuple(pltpu.VMEM(shape, jnp.float32) for shape in ((48, 16, 128), (72, 8, 128))),
         in_specs=[pl.BlockSpec(memory_space=pltpu.HBM)] * 2,
         out_specs=(pl.BlockSpec(memory_space=pltpu.VMEM),) * 2,
         scratch_shapes=[

time: 17.3 us -> 17.3 us (level)
  no operation moved by 1% of the time
where the time goes in v11:
time: 17.3 us; the launch traced here: 17.1 us
  Pallas kernels  16.4 us (95%)
  between operations  0.64 us (4%)
    pallas_call x1, Pallas kernels, body(): pl.pallas_call(kernel, out_shape=tuple((pltpu.VMEM(shape, jnp.float32) fo...  15.7 us
    pallas_call x1, Pallas kernels, body(): pl.pallas_call(store_kernel, out_shape=(jax.ShapeDtypeStruct(x.shape, jnp...  0.76 us

profile of v11, /device:TPU:23, one launch (start us, length us, event | category | flops | bytes accessed | tf_op | source)
XLA Modules:
  0.0 17.1 jit_solution(16352043476783878192)
XLA Ops:
  0.6 15.7 %shard_map.41 = (f32[48,16,128]{2,1,0:T(8,128)S(1)}, f32[72,8,128]{2,1,0:T(8,128)S(1)}) custom-call(f32[12,16,128]{2,1,0:T(8,128)} %bitcast.5, f32[36,16,128]{2,1,0:T(8,128)} %bitcast.4), custom_call_target="tpu_custom_call" | custom-call | flops 6000000 | bytes 800000 | tf_op jit(solution)/shard_map/pallas_call | solution.py:596
  16.3 0.8 %shard_map.42 = (f32[12,16,128]{2,1,0:T(8,128)}, f32[36,16,128]{2,1,0:T(8,128)}) custom-call(f32[48,16,128]{2,1,0:T(8,128)S(1)} %get-tuple-element.6.out_in, f32[72,8,128]{2,1,0:T(8,128)S(1)} %get-tuple-element.7.z_in), custom_call_target="tpu_custom_call" | custom-call | flops 400000 | bytes 800000 | tf_op jit(solution)/shard_map/pallas_call | solution.py:618

commit v12 on v11

--- a/solution.py
+++ b/solution.py
@@ -351,12 +351,14 @@
     z_and_y = pltpu.make_async_copy(outbox.at[pl.ds(0, 12)], inbox.at[pl.ds(0, 12)], recv_sem.at[RECV_SEM[Z_DIR, 0]])
     all_up = pltpu.make_async_copy(outbox.at[pl.ds(0, 15)], inbox.at[pl.ds(0, 15)], recv_sem.at[RECV_UP])
     all_sent = pltpu.make_async_copy(outbox, inbox, send_sem.at[0])
+    edge_rows = u_buf.at[pl.ds(0, 33), 0:12]
+    all_and_edges_sent = pltpu.make_async_copy(edge_rows, edge_rows, send_sem.at[0])
 
     def edge_link(d, src, dst):
         return pltpu.make_async_remote_copy(
             src_ref=src,
             dst_ref=dst,
-            send_sem=send_sem.at[1],
+            send_sem=send_sem.at[0],
             recv_sem=recv_sem.at[RECV_EDGE[d]],
             device_id={AXES[d]: behind[d], AXES[Y_DIR]: ahead[Y_DIR]},
             device_id_type=MESH,
@@ -366,7 +368,6 @@
         T_DIR: edge_link(T_DIR, edge_out, edge_t),
         Z_DIR: edge_link(Z_DIR, face_of(outbox, Y_DIR, 1).at[:, 0:2], edge_z.at[:, 6:8]),
     }
-    both_edges = edge_link(T_DIR, y_now.at[:, 0:6], y_now.at[:, 0:6])
 
     here = {T_DIR: here_sem.at[0], Z_DIR: here_sem.at[0], Y_DIR: here_sem.at[1]}
     here_near = here_sem.at[2]
@@ -562,9 +563,8 @@
             (tr - scale * er, ti - scale * ei) for (tr, ti), (er, ei) in zip(there, extra)
         ]
         finish(d, first[d], there)
-    all_sent.wait()
-
-    pl.when(is_last_y)(both_edges.wait_send)
+    pl.when(plain)(all_sent.wait)
+    pl.when(is_last_y)(all_and_edges_sent.wait)
 
 
 def store_kernel(out_in, z_in, y_out, f_out, fz_buf, sem):
@@ -608,7 +608,7 @@
             pltpu.VMEM((3, 8, 128), jnp.float32),
             pltpu.VMEM((6, 8, 128), jnp.float32),
             pltpu.SemaphoreType.DMA((2,)),
-            pltpu.SemaphoreType.DMA((2,)),
+            pltpu.SemaphoreType.DMA((1,)),
             pltpu.SemaphoreType.DMA((6,)),
             pltpu.SemaphoreType.REGULAR((3,)),
         ],

time: 17.3 us -> 17.2 us (level)
  no operation moved by 1% of the time
where the time goes in v12:
time: 17.2 us; the launch traced here: 17.1 us
  Pallas kernels  16.4 us (95%)
  between operations  0.64 us (4%)
    pallas_call x1, Pallas kernels, body(): pl.pallas_call(kernel, out_shape=tuple((pltpu.VMEM(shape, jnp.float32) fo...  15.7 us
    pallas_call x1, Pallas kernels, body(): pl.pallas_call(store_kernel, out_shape=(jax.ShapeDtypeStruct(x.shape, jnp...  0.76 us

profile of v12, /device:TPU:23, one launch (start us, length us, event | category | flops | bytes accessed | tf_op | source)
XLA Modules:
  0.0 17.1 jit_solution(2887377404098662144)
XLA Ops:
  0.6 15.7 %shard_map.41 = (f32[48,16,128]{2,1,0:T(8,128)S(1)}, f32[72,8,128]{2,1,0:T(8,128)S(1)}) custom-call(f32[12,16,128]{2,1,0:T(8,128)} %bitcast.5, f32[36,16,128]{2,1,0:T(8,128)} %bitcast.4), custom_call_target="tpu_custom_call" | custom-call | flops 6000000 | bytes 800000 | tf_op jit(solution)/shard_map/pallas_call | solution.py:596
  16.3 0.8 %shard_map.42 = (f32[12,16,128]{2,1,0:T(8,128)}, f32[36,16,128]{2,1,0:T(8,128)}) custom-call(f32[48,16,128]{2,1,0:T(8,128)S(1)} %get-tuple-element.6.out_in, f32[72,8,128]{2,1,0:T(8,128)S(1)} %get-tuple-element.7.z_in), custom_call_target="tpu_custom_call" | custom-call | flops 400000 | bytes 800000 | tf_op jit(solution)/shard_map/pallas_call | solution.py:618
